TPU v7x, 512 devices: a whole 4x8x8 slice. The times are simulated.
512 devices in a mesh: vol: 64 (over z_lo, y, core), strip: 8 (over z_hi, x).
Axes of the slice: x: 4, y: 8, z: 8 (z_hi: 2, z_lo: 4; z = z_hi * 4 + z_lo), core: 2. Of those that a mesh axis runs over, the one named last changes fastest.
Arguments:
- frames: bfloat16 [128, 1, 2048, 1024], P('vol', None, 'strip'), may hold values from 0.5 to 4
- kappa: float32 [128], P('vol'), may hold values from 0.3 to 3
Outputs:
- dff: bfloat16 [128, 1, 256, 8, 1024], P(None, None, 'vol', 'strip')
- slope: bfloat16 [128, 1, 256, 8, 1024], P(None, None, 'vol', 'strip')
All inputs are finite; a program needn't handle non-finite values.
Results may differ from a plain program's by a relative error of at most 0.0097.
Values may be sent and summed in bfloat16 or wider, within the bound.
No kernel may reach another device: no remote copies, remote signals or barrier semaphores. Data moves between devices by JAX's collectives and lax.ppermute only.
A program may use at most 64 MiB of HBM per device.

v0:
```python
import jax
import jax.numpy as jnp
from jax import lax
from jax.sharding import PartitionSpec as P

PASSES = 3
BAND = 16


def extended_2(value, sides, width):
    for axis, dim in sides:
        devices, length = (lax.axis_size(axis), value.shape[dim])
        up = [(i, (i + 1) % devices) for i in range(devices - 1)]
        down = [(j, i) for i, j in up]
        last = lax.slice_in_dim(value, length - width, length, axis=dim)
        first = lax.slice_in_dim(value, 0, width, axis=dim)
        before = lax.ppermute(last, axis, up)
        after = lax.ppermute(first, axis, down)
        value = jnp.concatenate([before, value, after], axis=dim)
    return value


def flux(diff, kap):
    ratio = diff / kap
    return diff / (1.0 + ratio * ratio)


def advance(extended, kap):
    center = extended[..., 1:-1, :]
    upper = extended[..., :-2, :] - center
    lower = extended[..., 2:, :] - center
    padded = jnp.pad(center, [(0, 0)] * (center.ndim - 1) + [(1, 1)])
    left = padded[..., :-2] - center
    right = padded[..., 2:] - center
    total = flux(upper, kap) + flux(lower, kap) + flux(left, kap) + flux(right, kap)
    return center + 0.2 * total


def smooth_weights(times):
    steps = jnp.arange(times, dtype=jnp.int32)
    gap = jnp.abs(steps[:, None] - steps[None, :])
    raw = jnp.where(gap <= BAND, BAND + 1 - gap, 0).astype(jnp.float32)
    return (raw / jnp.sum(raw, axis=1, keepdims=True)).astype(jnp.bfloat16)


def detrend(piece):
    times = piece.shape[0]
    weights = smooth_weights(times)
    flat = piece.reshape(times, -1)
    baseline = jnp.dot(weights, flat, preferred_element_type=jnp.float32)
    ratio = (flat.astype(jnp.float32) - baseline) / (baseline + 0.1)
    slope = jnp.concatenate(
        [ratio[1:2] - ratio[0:1], (ratio[2:] - ratio[:-2]) * 0.5, ratio[-1:] - ratio[-2:-1]], axis=0
    )
    return (
        ratio.reshape(piece.shape).astype(jnp.bfloat16),
        slope.reshape(piece.shape).astype(jnp.bfloat16),
    )


def local(frames, kappa):
    kap = kappa[:, None, None, None]
    field = frames.astype(jnp.float32)
    for step in range(PASSES):
        extended = extended_2(field, (("strip", 2),), 1)
        field = advance(extended, kap)
    stored = field.astype(jnp.bfloat16)
    ratio, slope = detrend(lax.all_to_all(stored, "vol", split_axis=2, concat_axis=0, tiled=True))
    return (ratio[:, :, :, None, :], slope[:, :, :, None, :])


def solution(mesh):
    placed = (P("vol", None, "strip", None), P("vol"))
    return jax.shard_map(
        local,
        mesh=mesh,
        in_specs=placed,
        out_specs=(P(None, None, "vol", "strip", None), P(None, None, "vol", "strip", None)),
        check_vma=False,
    )
```

profile of v0, /device:TPU:7, one launch (start us, length us, event | category | flops | bytes accessed | tf_op | source)
XLA Modules:
  0.0 106.4 jit_solution(1144931617588871949)
XLA Ops:
  0.6 0.0 copy-start
  0.6 0.0 copy-start.1
  0.7 0.9 fusion.23
  1.5 10.6 %collective-permute-start = (f32[2,1,1,1024]{3,2,1,0:T(1,128)S(1)}, f32[2,1,1,1024]{3,2,1,0:T(1,128)S(1)}, u32[]{:S(2)}, u32[]{:S(2)}) collective-permute-start(f32[2,1,1,1024]{3,2,1,0:T(1,128)S(1)} %get-tuple-element.20), channel_id=1, source_target_pairs={{0,1},{1,2},{2,3},{3,4},{4,5},{5,6},{6,7},{8,9},{9,10},{10,11},{11... | collective-permute-start | bytes 24584 | tf_op jit(solution)/shard_map/ppermute | solution.py:17
  12.1 1.9 %collective-permute-start.1 = (f32[2,1,1,1024]{3,2,1,0:T(1,128)S(1)}, f32[2,1,1,1024]{3,2,1,0:T(1,128)S(1)}, u32[]{:S(2)}, u32[]{:S(2)}) collective-permute-start(f32[2,1,1,1024]{3,2,1,0:T(1,128)S(1)} %get-tuple-element.21), channel_id=1, source_target_pairs={{1,0},{2,1},{3,2},{4,3},{5,4},{6,5},{7,6},{9,8},{10,9},{11,10},{12... | collective-permute-start | bytes 24584 | tf_op jit(solution)/shard_map/ppermute | solution.py:18
  14.0 1.5 %convert_element_type.49 = f32[2,1,256,1024]{3,2,1,0:T(8,128)S(1)} convert(bf16[2,1,256,1024]{3,2,1,0:T(8,128)(2,1)} %param.2) | non-fusion elementwise | flops 524288 | bytes 3145728 | tf_op jit(solution)/shard_map/convert_element_type | solution.py:63
  15.5 0.0 collective-permute-done
  15.5 7.0 %collective-permute-done.1 = f32[2,1,1,1024]{3,2,1,0:T(1,128)S(1)} collective-permute-done((f32[2,1,1,1024]{3,2,1,0:T(1,128)S(1)}, f32[2,1,1,1024]{3,2,1,0:T(1,128)S(1)}, u32[]{:S(2)}, u32[]{:S(2)}) %collective-permute-start.1) | collective-permute-done | bytes 8224 | tf_op jit(solution)/shard_map/ppermute | solution.py:18
  22.5 0.0 copy-done
  22.5 0.0 copy-done.1
  22.5 2.7 %convert_add_fusion = f32[2,1,256,1024]{3,2,1,0:T(8,128)S(1)} fusion(bf16[2,1,256,1024]{3,2,1,0:T(8,128)(2,1)S(1)} %copy-done, f32[2,1,256,1024]{3,2,1,0:T(8,128)S(1)} %convert_element_type.49, f32[2,1,1,1024]{3,2,1,0:T(1,128)S(1)} %collective-permute-done.1, f32[2,1,1,1024]{3,2,1,0:T(1,128)S(1)} %collective-permute-done, f32[2]{0:T(128)S(1)} %copy-done.1), kind=kLoop, calls=%fused_computation | loop fusion | flops 14680064 | bytes 5259272 | tf_op jit(solution)/shard_map/add | solution.py:36
  25.2 2.4 %collective-permute-start.2 = (f32[2,1,1,1024]{3,2,1,0:T(1,128)S(1)}, f32[2,1,1,1024]{3,2,1,0:T(1,128)S(1)}, u32[]{:S(2)}, u32[]{:S(2)}) collective-permute-start(f32[2,1,1,1024]{3,2,1,0:T(1,128)S(1)} %get-tuple-element.18), channel_id=1, source_target_pairs={{0,1},{1,2},{2,3},{3,4},{4,5},{5,6},{6,7},{8,9},{9,10},{10,11},{11... | collective-permute-start | bytes 24584 | tf_op jit(solution)/shard_map/ppermute | solution.py:17
  27.7 2.9 %collective-permute-start.3 = (f32[2,1,1,1024]{3,2,1,0:T(1,128)S(1)}, f32[2,1,1,1024]{3,2,1,0:T(1,128)S(1)}, u32[]{:S(2)}, u32[]{:S(2)}) collective-permute-start(f32[2,1,1,1024]{3,2,1,0:T(1,128)S(1)} %get-tuple-element.19), channel_id=1, source_target_pairs={{1,0},{2,1},{3,2},{4,3},{5,4},{6,5},{7,6},{9,8},{10,9},{11,10},{12... | collective-permute-start | bytes 24584 | tf_op jit(solution)/shard_map/ppermute | solution.py:18
  30.5 0.0 collective-permute-done.2
  30.5 7.5 %collective-permute-done.3 = f32[2,1,1,1024]{3,2,1,0:T(1,128)S(1)} collective-permute-done((f32[2,1,1,1024]{3,2,1,0:T(1,128)S(1)}, f32[2,1,1,1024]{3,2,1,0:T(1,128)S(1)}, u32[]{:S(2)}, u32[]{:S(2)}) %collective-permute-start.3) | collective-permute-done | bytes 8224 | tf_op jit(solution)/shard_map/ppermute | solution.py:18
  38.1 2.6 %multiply_add_fusion = f32[2,1,256,1024]{3,2,1,0:T(8,128)S(1)} fusion(f32[2,1,256,1024]{3,2,1,0:T(8,128)S(1)} %convert_add_fusion, f32[2,1,1,1024]{3,2,1,0:T(1,128)S(1)} %collective-permute-done.3, f32[2,1,1,1024]{3,2,1,0:T(1,128)S(1)} %collective-permute-done.2, f32[2]{0:T(128)S(1)} %copy-done.1), kind=kLoop, calls=%fused_computation.30 | loop fusion | flops 14155776 | bytes 4210696 | tf_op jit(solution)/shard_map/add | solution.py:36
  40.7 1.9 %collective-permute-start.4 = (f32[2,1,1,1024]{3,2,1,0:T(1,128)S(1)}, f32[2,1,1,1024]{3,2,1,0:T(1,128)S(1)}, u32[]{:S(2)}, u32[]{:S(2)}) collective-permute-start(f32[2,1,1,1024]{3,2,1,0:T(1,128)S(1)} %get-tuple-element.16), channel_id=1, source_target_pairs={{0,1},{1,2},{2,3},{3,4},{4,5},{5,6},{6,7},{8,9},{9,10},{10,11},{11... | collective-permute-start | bytes 24584 | tf_op jit(solution)/shard_map/ppermute | solution.py:17
  42.7 3.4 %collective-permute-start.5 = (f32[2,1,1,1024]{3,2,1,0:T(1,128)S(1)}, f32[2,1,1,1024]{3,2,1,0:T(1,128)S(1)}, u32[]{:S(2)}, u32[]{:S(2)}) collective-permute-start(f32[2,1,1,1024]{3,2,1,0:T(1,128)S(1)} %get-tuple-element.17), channel_id=1, source_target_pairs={{1,0},{2,1},{3,2},{4,3},{5,4},{6,5},{7,6},{9,8},{10,9},{11,10},{12... | collective-permute-start | bytes 24584 | tf_op jit(solution)/shard_map/ppermute | solution.py:18
  46.0 0.0 collective-permute-done.4
  46.1 7.0 %collective-permute-done.5 = f32[2,1,1,1024]{3,2,1,0:T(1,128)S(1)} collective-permute-done((f32[2,1,1,1024]{3,2,1,0:T(1,128)S(1)}, f32[2,1,1,1024]{3,2,1,0:T(1,128)S(1)}, u32[]{:S(2)}, u32[]{:S(2)}) %collective-permute-start.5) | collective-permute-done | bytes 8224 | tf_op jit(solution)/shard_map/ppermute | solution.py:18
  53.1 2.7 %add_convert_fusion = bf16[2,1,256,1024]{3,2,1,0:T(8,128)(2,1)S(1)} fusion(f32[2,1,256,1024]{3,2,1,0:T(8,128)S(1)} %multiply_add_fusion, f32[2,1,1,1024]{3,2,1,0:T(1,128)S(1)} %collective-permute-done.5, f32[2,1,1,1024]{3,2,1,0:T(1,128)S(1)} %collective-permute-done.4, f32[2]{0:T(128)S(1)} %copy-done.1), kind=kLoop, calls=%fused_computation.29 | loop fusion | flops 14680064 | bytes 3162120 | tf_op jit(solution)/shard_map/convert_element_type | solution.py:67
  55.8 2.0 %copy.41 = bf16[2,1,256,1024]{3,0,1,2:T(2,128)(2,1)} copy(bf16[2,1,256,1024]{3,2,1,0:T(8,128)(2,1)S(1)} %add_convert_fusion) | data formatting | bytes 2097152 | tf_op jit(solution)/shard_map/convert_element_type | solution.py:67
  57.8 14.3 %all-to-all-start = ((bf16[2,1,256,1024]{3,0,1,2:T(2,128)(2,1)}), bf16[2,1,256,1024]{3,0,1,2:T(2,128)(2,1)S(1)}, u32[]{:S(2)}, u32[]{:S(2)}) async-start(bf16[2,1,256,1024]{3,0,1,2:T(2,128)(2,1)} %copy.41), calls=%async_computation | async-start | bytes 2097152 | tf_op jit(solution)/shard_map/all_to_all | solution.py:68
  72.1 0.1 convert_reduce_fusion
  72.3 28.7 %all-to-all-done = bf16[2,1,256,1024]{3,0,1,2:T(2,128)(2,1)S(1)} async-done(((bf16[2,1,256,1024]{3,0,1,2:T(2,128)(2,1)}), bf16[2,1,256,1024]{3,0,1,2:T(2,128)(2,1)S(1)}, u32[]{:S(2)}, u32[]{:S(2)}) %all-to-all-start) | async-done | bytes 1048608 | tf_op jit(solution)/shard_map/all_to_all | solution.py:68
  101.0 0.5 copy.42
  101.5 0.4 copy.45
  101.9 0.7 fusion.24
  102.6 0.3 fusion.5
  102.9 1.6 %convert_element_type.55 = bf16[128,1,4,1,1024]{4,2,0,3,1:T(4,128)(2,1)} reshape(bf16[128,4096]{1,0:T(8,128)(2,1)S(1)} %get-tuple-element.22) | data formatting | bytes 2097152 | tf_op jit(solution)/shard_map/convert_element_type | solution.py:56
  104.5 0.3 pad_maximum_fusion.6
  104.8 1.6 %convert_element_type.56 = bf16[128,1,4,1,1024]{4,2,0,3,1:T(4,128)(2,1)} reshape(bf16[128,4096]{1,0:T(8,128)(2,1)S(1)} %pad_maximum_fusion.6) | data formatting | bytes 2097152 | tf_op jit(solution)/shard_map/convert_element_type | solution.py:57
  (3 shorter events, 0.1 us)
Async XLA Ops:
  0.6 21.9 %copy-start = (bf16[2,1,256,1024]{3,2,1,0:T(8,128)(2,1)S(1)}, bf16[2,1,256,1024]{3,2,1,0:T(8,128)(2,1)}, u32[]{:S(2)}) copy-start(bf16[2,1,256,1024]{3,2,1,0:T(8,128)(2,1)} %param.2) | copy-start | bytes 3145732
  0.6 21.9 %copy-start.1 = (f32[2]{0:T(128)S(1)}, f32[2]{0:T(128)}, u32[]{:S(2)}) copy-start(f32[2]{0:T(128)} %param.3) | copy-start | bytes 28
  1.5 14.0 %collective-permute-start = (f32[2,1,1,1024]{3,2,1,0:T(1,128)S(1)}, f32[2,1,1,1024]{3,2,1,0:T(1,128)S(1)}, u32[]{:S(2)}, u32[]{:S(2)}) collective-permute-start(f32[2,1,1,1024]{3,2,1,0:T(1,128)S(1)} %get-tuple-element.20), channel_id=1, source_target_pairs={{0,1},{1,2},{2,3},{3,4},{4,5},{5,6},{6,7},{8,9},{9,10},{10,11},{11... | collective-permute-start | bytes 24584 | tf_op jit(solution)/shard_map/ppermute | solution.py:17
  12.1 10.4 %collective-permute-start.1 = (f32[2,1,1,1024]{3,2,1,0:T(1,128)S(1)}, f32[2,1,1,1024]{3,2,1,0:T(1,128)S(1)}, u32[]{:S(2)}, u32[]{:S(2)}) collective-permute-start(f32[2,1,1,1024]{3,2,1,0:T(1,128)S(1)} %get-tuple-element.21), channel_id=1, source_target_pairs={{1,0},{2,1},{3,2},{4,3},{5,4},{6,5},{7,6},{9,8},{10,9},{11,10},{12... | collective-permute-start | bytes 24584 | tf_op jit(solution)/shard_map/ppermute | solution.py:18
  25.2 5.3 %collective-permute-start.2 = (f32[2,1,1,1024]{3,2,1,0:T(1,128)S(1)}, f32[2,1,1,1024]{3,2,1,0:T(1,128)S(1)}, u32[]{:S(2)}, u32[]{:S(2)}) collective-permute-start(f32[2,1,1,1024]{3,2,1,0:T(1,128)S(1)} %get-tuple-element.18), channel_id=1, source_target_pairs={{0,1},{1,2},{2,3},{3,4},{4,5},{5,6},{6,7},{8,9},{9,10},{10,11},{11... | collective-permute-start | bytes 24584 | tf_op jit(solution)/shard_map/ppermute | solution.py:17
  27.7 10.4 %collective-permute-start.3 = (f32[2,1,1,1024]{3,2,1,0:T(1,128)S(1)}, f32[2,1,1,1024]{3,2,1,0:T(1,128)S(1)}, u32[]{:S(2)}, u32[]{:S(2)}) collective-permute-start(f32[2,1,1,1024]{3,2,1,0:T(1,128)S(1)} %get-tuple-element.19), channel_id=1, source_target_pairs={{1,0},{2,1},{3,2},{4,3},{5,4},{6,5},{7,6},{9,8},{10,9},{11,10},{12... | collective-permute-start | bytes 24584 | tf_op jit(solution)/shard_map/ppermute | solution.py:18
  40.7 5.3 %collective-permute-start.4 = (f32[2,1,1,1024]{3,2,1,0:T(1,128)S(1)}, f32[2,1,1,1024]{3,2,1,0:T(1,128)S(1)}, u32[]{:S(2)}, u32[]{:S(2)}) collective-permute-start(f32[2,1,1,1024]{3,2,1,0:T(1,128)S(1)} %get-tuple-element.16), channel_id=1, source_target_pairs={{0,1},{1,2},{2,3},{3,4},{4,5},{5,6},{6,7},{8,9},{9,10},{10,11},{11... | collective-permute-start | bytes 24584 | tf_op jit(solution)/shard_map/ppermute | solution.py:17
  42.7 10.4 %collective-permute-start.5 = (f32[2,1,1,1024]{3,2,1,0:T(1,128)S(1)}, f32[2,1,1,1024]{3,2,1,0:T(1,128)S(1)}, u32[]{:S(2)}, u32[]{:S(2)}) collective-permute-start(f32[2,1,1,1024]{3,2,1,0:T(1,128)S(1)} %get-tuple-element.17), channel_id=1, source_target_pairs={{1,0},{2,1},{3,2},{4,3},{5,4},{6,5},{7,6},{9,8},{10,9},{11,10},{12... | collective-permute-start | bytes 24584 | tf_op jit(solution)/shard_map/ppermute | solution.py:18
  57.8 43.1 %all-to-all-start = ((bf16[2,1,256,1024]{3,0,1,2:T(2,128)(2,1)}), bf16[2,1,256,1024]{3,0,1,2:T(2,128)(2,1)S(1)}, u32[]{:S(2)}, u32[]{:S(2)}) async-start(bf16[2,1,256,1024]{3,0,1,2:T(2,128)(2,1)} %copy.41), calls=%async_computation | async-start | bytes 2097152 | tf_op jit(solution)/shard_map/all_to_all | solution.py:68
where the time goes:
time: 107 us; the launch traced here: 106 us
  waiting for transfers between devices  50.3 us (47%)
  starting transfers between devices  37.3 us (35%)
  other arithmetic  10.3 us (10%)
  local copies, waits for them, and re-layouts  7.04 us (7%)
    all_to_all x1, waiting for transfers between devices, local(): lax.all_to_all(stored, 'vol', split_axis=2, concat_axis=0, tiled=True)  28.7 us
    ppermute x3, waiting for transfers between devices, extended_2(): after = lax.ppermute(first, axis, down)  21.6 us
    ppermute x3, starting transfers between devices, extended_2(): before = lax.ppermute(last, axis, up)  14.9 us
    all_to_all x1, starting transfers between devices, local(): lax.all_to_all(stored, 'vol', split_axis=2, concat_axis=0, tiled=True)  14.3 us
    ppermute x3, starting transfers between devices, extended_2(): after = lax.ppermute(first, axis, down)  8.16 us
    add x2, other arithmetic, advance(): return center + 0.2 * total  5.34 us
    convert_element_type x1, other arithmetic, local(): stored = field.astype(jnp.bfloat16)  2.7 us
  transfers between devices with their start and end apart: 7, of which 4 were waited for; matrix products, arithmetic and copies ran while one was open for 1% of the time, Pallas kernels for 0%

commit v1 on v0

v1 whole, which is shorter than its diff:
```python
import functools
import math
import numpy as np
import jax
import jax.numpy as jnp
from jax import lax
from jax.experimental import pallas as pl
from jax.experimental.pallas import tpu as pltpu
from jax.sharding import PartitionSpec as P

PASSES = 3
BAND = 16
TIMES = 128
LANES = 128
TILES = 8
ROWS = 256
HALO = 4
STEP = 16
STARTS = (0, 64, 192, 256)
CHUNK = 256
ROOT5 = math.sqrt(5.0)


def band_weights():
    steps = np.arange(TIMES)
    gap = np.abs(steps[:, None] - steps[None, :])
    raw = np.where(gap <= BAND, BAND + 1 - gap, 0).astype(np.float32)
    weights = raw / np.sum(raw, axis=1, keepdims=True, dtype=np.float32)
    spread = np.kron(weights, np.eye(4, dtype=np.float32))
    blocks = [spread[128 * b : 128 * b + 128, k : k + 256] for b, k in enumerate(STARTS)]
    return jnp.asarray(np.concatenate(blocks, axis=0), jnp.bfloat16)


def flux(diff):
    return diff * pl.reciprocal(5.0 + diff * diff, approx=True)


def advance(mid, below, carry):
    shape = mid[0][0].shape
    lane = lax.broadcasted_iota(jnp.int32, shape, 1)
    row = lax.broadcasted_iota(jnp.int32, shape, 0)
    last, first, top = lane == LANES - 1, lane == 0, row == 0
    carry = list(carry)
    new = []
    for k, pieces in enumerate(mid):
        line = []
        turned = pltpu.roll(pieces[0], LANES - 1, 1)
        before = flux(pieces[0])
        for i, value in enumerate(pieces):
            later = pltpu.roll(pieces[i + 1], LANES - 1, 1) if i + 1 < len(pieces) else jnp.zeros_like(value)
            right = flux(jnp.where(last, later, turned) - value)
            turned = later
            moved = pltpu.roll(right, 1, 1)
            left = jnp.where(first, before, moved)
            before = moved
            down = flux(below[k][i] - value)
            sunk = pltpu.roll(down, 1, 0)
            up = jnp.where(top, carry[i], sunk)
            carry[i] = sunk
            line.append(value + ((down - up) + (right - left)))
        new.append(line)
    return new, carry


def inner_kernel(kappa_ref, frames_ref, out_ref, field):
    for v in range(2):
        unit = ROOT5 / jnp.full((STEP, LANES), kappa_ref[v], jnp.float32)

        def load(j, _, v=v, unit=unit):
            at = pl.multiple_of(j * STEP, STEP)
            for i in range(TILES):
                value = frames_ref[v, pl.ds(at, STEP), i * LANES : (i + 1) * LANES]
                field[v, i, pl.ds(at, STEP), :] = value.astype(jnp.float32) * unit
            return 0

        lax.fori_loop(0, ROWS // STEP, load, 0)
        for i in range(TILES):
            field[v, i, ROWS : ROWS + 8, :] = jnp.zeros((8, LANES), jnp.float32)

    zero = jnp.zeros((8, LANES), jnp.float32)

    def read(v, at):
        mid = [[field[v, i, pl.ds(at + 8 * k, 8), :] for i in range(TILES)] for k in range(STEP // 8)]
        below = [[field[v, i, pl.ds(at + 8 * k + 1, 8), :] for i in range(TILES)] for k in range(STEP // 8)]
        return mid, below

    for p in range(PASSES - 1):

        def step(j, carry):
            at = pl.multiple_of(j * STEP, STEP)
            later = []
            for v in range(2):
                mid, below = read(v, at)
                new, after = advance(mid, below, carry[v])
                for k in range(STEP // 8):
                    for i in range(TILES):
                        field[v, i, pl.ds(at + 8 * k, 8), :] = new[k][i]
                later.append(after)
            return later

        lax.fori_loop(0, ROWS // STEP, step, [[zero] * TILES] * 2)

    units = [jnp.full((8, LANES), kappa_ref[v], jnp.float32) * (1.0 / ROOT5) for v in range(2)]
    low = lax.broadcasted_iota(jnp.int32, (8, LANES), 0) < 4

    def step(j, carry):
        at = pl.multiple_of(j * STEP, STEP)
        later, both = [], []
        for v in range(2):
            mid, below = read(v, at)
            new, after = advance(mid, below, carry[v])
            later.append(after)
            both.append(new)
        for k in range(STEP // 8):
            for i in range(TILES):
                a, b = both[0][k][i] * units[0], both[1][k][i] * units[1]
                even = jnp.where(low, a, pltpu.roll(b, 4, 0))
                odd = jnp.where(low, pltpu.roll(a, 4, 0), b)
                spot = j * (STEP // 8) + k
                out_ref[spot, 0, :, i * LANES : (i + 1) * LANES] = even.astype(jnp.bfloat16)
                out_ref[spot, 1, :, i * LANES : (i + 1) * LANES] = odd.astype(jnp.bfloat16)
        return later

    lax.fori_loop(0, ROWS // STEP, step, [[zero] * TILES] * 2)


def edge_kernel(kappa_ref, head_ref, tail_ref, above_ref, under_ref, _, out_ref, sems, field, blocks):
    strip = lax.axis_index("strip")
    inside = (
        jnp.where(strip == 0, 0.0, 1.0).astype(jnp.float32),
        jnp.where(strip == lax.axis_size("strip") - 1, 0.0, 1.0).astype(jnp.float32),
    )
    low = lax.broadcasted_iota(jnp.int32, (8, LANES), 0) < 4
    zero = jnp.zeros((8, LANES), jnp.float32)
    spots = [slice(i * LANES, (i + 1) * LANES) for i in range(TILES)]
    done = []
    for v in range(2):
        unit = ROOT5 / jnp.full((1, LANES), kappa_ref[v], jnp.float32)
        sides = []
        for side in range(2):
            if side == 0:
                own = head_ref[v].astype(jnp.float32)[0:8]
                far = above_ref[v].astype(jnp.float32)
                window = [jnp.concatenate([far, far], axis=0), own]
            else:
                own = tail_ref[v].astype(jnp.float32)[8:16]
                far = under_ref[v].astype(jnp.float32)
                window = [own, jnp.concatenate([far, far], axis=0)]
            mid = [[w[:, s] * unit for s in spots] for w in window]
            for p in range(PASSES):
                for k in range(2):
                    for i in range(TILES):
                        field[2 * v + side, i, 8 * k : 8 * k + 8, :] = mid[k][i]
                below = [[field[2 * v + side, i, 8 * k + 1 : 8 * k + 9, :] for i in range(TILES)] for k in range(2)]
                mid, _unused = advance(mid, below, [zero] * TILES)
                mid[side] = [value * inside[side] for value in mid[side]]
            sides.append([value * (kappa_ref[v] * (1.0 / ROOT5)) for value in mid[1 - side]])
        done.append(sides)
    for i in range(TILES):
        top = jnp.where(low, done[0][0][i], pltpu.roll(done[1][0][i], 4, 0))
        end = jnp.where(low, pltpu.roll(done[0][1][i], 4, 0), done[1][1][i])
        blocks[0, :, spots[i]] = top.astype(jnp.bfloat16)
        blocks[1, :, spots[i]] = end.astype(jnp.bfloat16)
    copies = [
        pltpu.make_async_copy(blocks.at[0], out_ref.at[0, 0], sems.at[0]),
        pltpu.make_async_copy(blocks.at[1], out_ref.at[31, 1], sems.at[1]),
    ]
    for copy in copies:
        copy.start()
    for copy in copies:
        copy.wait()


def detrend_kernel(weights_ref, stored_ref, dff_ref, slope_ref, ratio):
    stored = stored_ref[...].reshape(4 * TIMES, CHUNK)
    for b, k in enumerate(STARTS):
        baseline = jnp.dot(
            weights_ref[128 * b : 128 * b + 128, :], stored[k : k + 256], preferred_element_type=jnp.float32
        )
        value = stored[128 * b : 128 * b + 128].astype(jnp.float32)
        ratio[16 * b : 16 * b + 16] = ((value - baseline) / (baseline + 0.1)).reshape(16, 8, CHUNK)

    low = lax.broadcasted_iota(jnp.int32, (8, LANES), 0) < 4
    for i in range(CHUNK // LANES):
        spot = slice(i * LANES, (i + 1) * LANES)
        own = ratio[0, :, spot]
        turned = pltpu.roll(own, 4, 0)
        previous = None
        for j in range(TIMES // 2):
            if j + 1 < TIMES // 2:
                other = ratio[j + 1, :, spot]
                other_turned = pltpu.roll(other, 4, 0)
                between = jnp.where(low, turned, other_turned)
            else:
                other = other_turned = None
                between = turned
            if previous is None:
                slope = jnp.where(low, between - own, 0.5 * (between - turned))
            elif other is None:
                slope = jnp.where(low, 0.5 * (between - previous), own - previous)
            else:
                slope = 0.5 * (between - previous)
            dff_ref[j, 0, :, spot] = own[0:4].astype(jnp.bfloat16)
            dff_ref[j, 1, :, spot] = turned[0:4].astype(jnp.bfloat16)
            slope_ref[j, 0, :, spot] = slope[0:4].astype(jnp.bfloat16)
            slope_ref[j, 1, :, spot] = pltpu.roll(slope, 4, 0)[0:4].astype(jnp.bfloat16)
            own, turned, previous = other, other_turned, between


VMEM = pl.BlockSpec(memory_space=pltpu.VMEM)
SMEM = pl.BlockSpec(memory_space=pltpu.SMEM)
ANY = pl.BlockSpec(memory_space=pl.ANY)


def diffuse(frames, kappa):
    devices = lax.axis_size("strip")
    up = [(i, i + 1) for i in range(devices - 1)]
    down = [(i + 1, i) for i in range(devices - 1)]
    above = lax.ppermute(frames[:, ROWS - HALO :], "strip", up)
    under = lax.ppermute(frames[:, :HALO], "strip", down)
    params = pltpu.CompilerParams(vmem_limit_bytes=24 * 1024 * 1024)
    inner = pl.pallas_call(
        inner_kernel,
        out_shape=jax.ShapeDtypeStruct((32, 2, 8, 1024), jnp.bfloat16),
        in_specs=[SMEM, VMEM],
        out_specs=VMEM,
        scratch_shapes=[pltpu.VMEM((2, TILES, ROWS + 8, LANES), jnp.float32)],
        compiler_params=params,
        cost_estimate=pl.CostEstimate(flops=60_000_000, bytes_accessed=2 << 20, transcendentals=3 << 20),
        name="inner",
    )(kappa, frames)
    whole = pl.pallas_call(
        edge_kernel,
        grid=(1,),
        out_shape=jax.ShapeDtypeStruct((32, 2, 8, 1024), jnp.bfloat16),
        in_specs=[
            SMEM,
            pl.BlockSpec((2, 16, 1024), lambda i: (0, 0, 0)),
            pl.BlockSpec((2, 16, 1024), lambda i: (0, 15, 0)),
            pl.BlockSpec((2, HALO, 1024), lambda i: (0, 0, 0)),
            pl.BlockSpec((2, HALO, 1024), lambda i: (0, 0, 0)),
            ANY,
        ],
        out_specs=ANY,
        scratch_shapes=[
            pltpu.SemaphoreType.DMA((2,)),
            pltpu.VMEM((4, TILES, 24, LANES), jnp.float32),
            pltpu.VMEM((2, 8, 1024), jnp.bfloat16),
        ],
        input_output_aliases={5: 0},
        compiler_params=params,
        name="edges",
    )(kappa, frames, frames, above, under, inner)
    return whole.reshape(64, 8, 1024)


def detrend(stored):
    block = pl.BlockSpec((64, 2, 4, CHUNK), lambda i: (0, 0, 0, i))
    shape = jax.ShapeDtypeStruct((64, 2, 4, 1024), jnp.bfloat16)
    return pl.pallas_call(
        detrend_kernel,
        grid=(1024 // CHUNK,),
        out_shape=[shape, shape],
        in_specs=[pl.BlockSpec((512, 256), lambda i: (0, 0)), pl.BlockSpec((64, 8, CHUNK), lambda i: (0, 0, i))],
        out_specs=[block, block],
        scratch_shapes=[pltpu.VMEM((64, 8, CHUNK), jnp.float32)],
        compiler_params=pltpu.CompilerParams(vmem_limit_bytes=24 * 1024 * 1024),
        name="detrend",
    )(band_weights(), stored)


def local(frames, kappa):
    blocks = diffuse(frames.reshape(2, ROWS, 1024), kappa)
    stored = lax.all_to_all(blocks, "vol", split_axis=0, concat_axis=0, tiled=True)
    dff, slope = detrend(stored)
    return dff.reshape(128, 1, 4, 1, 1024), slope.reshape(128, 1, 4, 1, 1024)


def solution(mesh):
    out = P(None, None, "vol", "strip", None)
    return jax.shard_map(
        local,
        mesh=mesh,
        in_specs=(P("vol", None, "strip", None), P("vol")),
        out_specs=(out, out),
        check_vma=False,
    )
```

time: 107 us -> 71.7 us (0.67)
  waiting for transfers between devices: 50.3 us -> 0.01 us
  blocking collectives: 0 us -> 41.9 us
  starting transfers between devices: 37.3 us -> 12.5 us
  Pallas kernels: 0 us -> 14.3 us
  other arithmetic: 10.3 us -> 0 us
  local copies, waits for them, and re-layouts: 7.04 us -> 2.03 us
    all_to_all x0 -> x1, blocking collectives: none -> 41.9 us  [local(): lax.all_to_all(blocks, 'vol', split_axis=0, concat_axis=0, tiled=True)]
    all_to_all x1 -> x0, waiting for transfers between devices: 28.7 us -> none  [local(): lax.all_to_all(stored, 'vol', split_axis=2, concat_axis=0, tiled=True)]
    ppermute x6 -> x2, waiting for transfers between devices: 21.6 us -> 0.01 us  [the longest x1 0.01 us: diffuse(): under = lax.ppermute(frames[:, :HALO], 'strip', down)]
    pallas_call x0 -> x3, Pallas kernels: none -> 14.3 us  [the longest x1 10.1 us: diffuse(): pl.pallas_call(inner_kernel, out_shape=jax.ShapeDtypeStruct((32, 2, 8, 10...]
    all_to_all x1 -> x0, starting transfers between devices: 14.3 us -> none  [local(): lax.all_to_all(stored, 'vol', split_axis=2, concat_axis=0, tiled=True)]
    ppermute x6 -> x2, starting transfers between devices: 23 us -> 12.5 us  [the longest x1 10 us: diffuse(): above = lax.ppermute(frames[:, ROWS - HALO:], 'strip', up)]
    add x2 -> x0, other arithmetic: 5.34 us -> none  [advance(): return center + 0.2 * total]
    convert_element_type x3 -> x0, local copies, waits for them, and re-layouts: 5.22 us -> none  [the longest x1 2.05 us: local(): stored = field.astype(jnp.bfloat16)]
  transfers between devices with their start and end apart: 7 -> 2, of which waited for: 4 -> 0; matrix products, arithmetic and copies ran while one was open for 1% -> 0% of each run, Pallas kernels for 0% -> 14%
where the time goes in v1:
time: 71.7 us; the launch traced here: 71.4 us
  blocking collectives  41.9 us (58%)
  Pallas kernels  14.3 us (20%)
  starting transfers between devices  12.5 us (17%)
  local copies, waits for them, and re-layouts  2.03 us (3%)
    all_to_all x1, blocking collectives, local(): lax.all_to_all(blocks, 'vol', split_axis=0, concat_axis=0, tiled=True)  41.9 us
    pallas_call x1, Pallas kernels, diffuse(): pl.pallas_call(inner_kernel, out_shape=jax.ShapeDtypeStruct((32, 2, 8, 10...  10.1 us
    ppermute x1, starting transfers between devices, diffuse(): above = lax.ppermute(frames[:, ROWS - HALO:], 'strip', up)  10 us
    pallas_call x1, Pallas kernels, detrend(): pl.pallas_call(detrend_kernel, grid=(1024 // CHUNK,), out_shape=[shape, s...  2.93 us
    ppermute x1, starting transfers between devices, diffuse(): under = lax.ppermute(frames[:, :HALO], 'strip', down)  2.46 us
  transfers between devices with their start and end apart: 2, of which 0 were waited for; matrix products, arithmetic and copies ran while one was open for 0% of the time, Pallas kernels for 14%

profile of v1, /device:TPU:7, one launch (start us, length us, event | category | flops | bytes accessed | tf_op | source)
XLA Modules:
  0.0 71.4 jit_solution(7673713378355498564)
XLA Ops:
  0.6 0.8 %fusion = (bf16[2,4,1024]{2,1,0:T(4,128)(2,1)S(1)}, bf16[2,4,1024]{2,1,0:T(4,128)(2,1)S(1)}) fusion(bf16[2,256,1024]{2,1,0:T(8,128)(2,1)} %bitcast.8), kind=kLoop, calls=%fused_computation | loop fusion | bytes 65536 | tf_op jit(solution)/shard_map/slice | solution.py:220
  1.4 0.0 copy-start.2
  1.4 2.5 %collective-permute-start.1 = (bf16[2,4,1024]{2,1,0:T(4,128)(2,1)S(1)}, bf16[2,4,1024]{2,1,0:T(4,128)(2,1)S(1)}, u32[]{:S(2)}, u32[]{:S(2)}) collective-permute-start(bf16[2,4,1024]{2,1,0:T(4,128)(2,1)S(1)} %get-tuple-element.8), channel_id=1, source_target_pairs={{1,0},{2,1},{3,2},{4,3},{5,4},{6,5},{7,6},{9,8},{10,9},{11,10},{12... | collective-permute-start | bytes 49160 | tf_op jit(solution)/shard_map/ppermute | solution.py:220
  3.9 10.0 %collective-permute-start = (bf16[2,4,1024]{2,1,0:T(4,128)(2,1)S(1)}, bf16[2,4,1024]{2,1,0:T(4,128)(2,1)S(1)}, u32[]{:S(2)}, u32[]{:S(2)}) collective-permute-start(bf16[2,4,1024]{2,1,0:T(4,128)(2,1)S(1)} %get-tuple-element.9), channel_id=1, source_target_pairs={{0,1},{1,2},{2,3},{3,4},{4,5},{5,6},{6,7},{8,9},{9,10},{10,11},{11... | collective-permute-start | bytes 49160 | tf_op jit(solution)/shard_map/ppermute | solution.py:219
  13.9 0.0 copy-done.2
  13.9 0.0 copy-start
  13.9 1.2 %copy-done = bf16[2,1,256,1024]{3,2,1,0:T(8,128)(2,1)S(1)} copy-done((bf16[2,1,256,1024]{3,2,1,0:T(8,128)(2,1)S(1)}, bf16[2,1,256,1024]{3,2,1,0:T(8,128)(2,1)}, u32[]{:S(2)}) %copy-start) | copy-done | bytes 1048600
  15.2 10.1 %inner.1._ = bf16[32,2,8,1024]{3,2,1,0:T(8,128)(2,1)S(1)} custom-call(f32[2]{0:T(128)S(1)} %copy-done.2, bf16[2,256,1024]{2,1,0:T(8,128)(2,1)S(1)} %bitcast.9), custom_call_target="tpu_custom_call" | custom-call | flops 60000000 | bytes 2097152 | tf_op jit(solution)/shard_map/inner/pallas_call | solution.py:222
  25.3 0.0 collective-permute-done.1.under_ref
  25.3 0.0 collective-permute-done.above_ref
  25.3 1.3 %edges.1 = bf16[32,2,8,1024]{3,2,1,0:T(8,128)(2,1)S(1)} custom-call(f32[2]{0:T(128)S(1)} %copy-done.2, bf16[2,256,1024]{2,1,0:T(8,128)(2,1)S(1)} %bitcast.10, bf16[2,256,1024]{2,1,0:T(8,128)(2,1)S(1)} %bitcast.11, bf16[2,4,1024]{2,1,0:T(4,128)(2,1)S(1)} %collective-permute-done.above_ref, ...), custom_call_target="tpu_custom_call", output_to_operand_aliasing={{}: (5, {})} | custom-call | tf_op jit(solution)/shard_map/edges/pallas_call | solution.py:232
  26.6 0.0 copy-start.1
  26.6 41.9 %all_to_all.5.stored_ref = bf16[64,8,1024]{2,1,0:T(8,128)(2,1)S(1)} all-to-all(bf16[64,8,1024]{2,1,0:T(8,128)(2,1)S(1)} %bitcast.12), channel_id=1, replica_groups=mesh['vol'=64,'strip'=8] {'vol'}, dimensions={0} | all-to-all | bytes 2097152 | tf_op jit(solution)/shard_map/all_to_all | solution.py:274
  68.5 0.0 copy-done.1
  68.5 2.9 %detrend.1 = (bf16[64,2,4,1024]{3,2,1,0:T(4,128)(2,1)}, bf16[64,2,4,1024]{3,2,1,0:T(4,128)(2,1)}) custom-call(bf16[512,256]{1,0:T(8,128)(2,1)S(1)} %copy-done.1, bf16[64,8,1024]{2,1,0:T(8,128)(2,1)S(1)} %all_to_all.5.stored_ref), custom_call_target="tpu_custom_call" | custom-call | tf_op jit(solution)/shard_map/detrend/pallas_call | solution.py:260
Async XLA Ops:
  1.4 12.5 %copy-start.2 = (f32[2]{0:T(128)S(1)}, f32[2]{0:T(128)}, u32[]{:S(2)}) copy-start(f32[2]{0:T(128)} %kappa_ref.3) | copy-start | bytes 28
  1.4 23.8 %collective-permute-start.1 = (bf16[2,4,1024]{2,1,0:T(4,128)(2,1)S(1)}, bf16[2,4,1024]{2,1,0:T(4,128)(2,1)S(1)}, u32[]{:S(2)}, u32[]{:S(2)}) collective-permute-start(bf16[2,4,1024]{2,1,0:T(4,128)(2,1)S(1)} %get-tuple-element.8), channel_id=1, source_target_pairs={{1,0},{2,1},{3,2},{4,3},{5,4},{6,5},{7,6},{9,8},{10,9},{11,10},{12... | collective-permute-start | bytes 49160 | tf_op jit(solution)/shard_map/ppermute | solution.py:220
  3.9 21.4 %collective-permute-start = (bf16[2,4,1024]{2,1,0:T(4,128)(2,1)S(1)}, bf16[2,4,1024]{2,1,0:T(4,128)(2,1)S(1)}, u32[]{:S(2)}, u32[]{:S(2)}) collective-permute-start(bf16[2,4,1024]{2,1,0:T(4,128)(2,1)S(1)} %get-tuple-element.9), channel_id=1, source_target_pairs={{0,1},{1,2},{2,3},{3,4},{4,5},{5,6},{6,7},{8,9},{9,10},{10,11},{11... | collective-permute-start | bytes 49160 | tf_op jit(solution)/shard_map/ppermute | solution.py:219
  13.9 1.2 %copy-start = (bf16[2,1,256,1024]{3,2,1,0:T(8,128)(2,1)S(1)}, bf16[2,1,256,1024]{3,2,1,0:T(8,128)(2,1)}, u32[]{:S(2)}) copy-start(bf16[2,1,256,1024]{3,2,1,0:T(8,128)(2,1)} %param.3) | copy-start | bytes 3145732
  26.6 41.9 %copy-start.1 = (bf16[512,256]{1,0:T(8,128)(2,1)S(1)}, bf16[512,256]{1,0:T(8,128)(2,1)}, u32[]{:S(2)}) copy-start(bf16[512,256]{1,0:T(8,128)(2,1)} %constant.2.clone.weights_ref) | copy-start | bytes 786436

commit v2 on v1

v2 whole, which is shorter than its diff:
```python
import functools
import math
import numpy as np
import jax
import jax.numpy as jnp
from jax import lax
from jax.experimental import pallas as pl
from jax.experimental.pallas import tpu as pltpu
from jax.sharding import PartitionSpec as P

PASSES = 3
BAND = 16
TIMES = 128
LANES = 128
TILES = 8
ROWS = 256
HALO = 4
GROUP = 4
WIDE = GROUP * LANES
MIX = 64
STARTS = (0, 64, 192, 256)
CHUNK = 512
ROOT5 = math.sqrt(5.0)


def band_weights():
    steps = np.arange(TIMES)
    gap = np.abs(steps[:, None] - steps[None, :])
    raw = np.where(gap <= BAND, BAND + 1 - gap, 0).astype(np.float32)
    weights = raw / np.sum(raw, axis=1, keepdims=True, dtype=np.float32)
    spread = np.kron(weights, np.eye(4, dtype=np.float32))
    blocks = [spread[128 * b : 128 * b + 128, k : k + 256] for b, k in enumerate(STARTS)]
    return jnp.asarray(np.concatenate(blocks, axis=0), jnp.bfloat16)


def flux(diff):
    return diff * pl.reciprocal(5.0 + diff * diff, approx=True)


def advance(pieces, below, above_flow, group):
    shape = pieces[0].shape
    lane = lax.broadcasted_iota(jnp.int32, shape, 1)
    last, first = lane == LANES - 1, lane == 0
    new = []
    before = flux(pieces[0])
    turned = pltpu.roll(pieces[0], LANES - 1, 1)
    for g in range(0, TILES, group):
        later = pltpu.roll(pieces[g + group], LANES - 1, 1) if g + group < TILES else jnp.zeros(shape, jnp.float32)
        right = list(pieces[g + 1 : g + group]) + [jnp.where(last, later, turned)]
        turned = later
        flow = [flux(right[t] - pieces[g + t]) for t in range(group)]
        moved = pltpu.roll(flow[-1], 1, 1)
        left = [jnp.where(first, before, moved)] + flow[:-1]
        before = moved
        for t in range(group):
            i = g + t
            down = flux(below[i] - pieces[i])
            up = above_flow(i, down)
            new.append(pieces[i] + ((down - up) + (flow[t] - left[t])))
    return new


def inner_kernel(kappa_ref, frames_ref, out_ref, ends_ref, field, flows, spread, gather, packed):
    source = lax.broadcasted_iota(jnp.int32, (WIDE, LANES), 0)
    lane = lax.broadcasted_iota(jnp.int32, (WIDE, LANES), 1)
    for t in range(GROUP):
        spread[:, t * LANES : (t + 1) * LANES] = (source == lane * GROUP + t).astype(jnp.float32).astype(jnp.bfloat16)
        place = (source & (LANES - 1)) * GROUP + lax.shift_right_logical(source, 7)
        gather[:, t * LANES : (t + 1) * LANES] = (place == lane + t * LANES).astype(jnp.float32).astype(jnp.bfloat16)
    units = [ROOT5 / jnp.full((8, LANES), kappa_ref[v], jnp.float32) for v in range(2)]
    backs = [jnp.full((8, LANES), kappa_ref[v], jnp.float32) * (1.0 / ROOT5) for v in range(2)]
    low = lax.broadcasted_iota(jnp.int32, (8, LANES), 0) < 4
    zero = jnp.zeros((8, LANES), jnp.float32)
    groups = TILES // GROUP
    for v in range(2):
        for i in range(TILES):
            field[v, i, ROWS : ROWS + 8, :] = zero
            flows[v, i, 0:8, :] = zero

    def fill(at):
        rows = [frames_ref[v, at : at + MIX, g * WIDE : (g + 1) * WIDE] for v in range(2) for g in range(groups)]
        value = jnp.dot(jnp.concatenate(rows, axis=0), spread[...], preferred_element_type=jnp.float32)
        for v in range(2):
            for i in range(TILES):
                g, t = i // GROUP, i % GROUP
                start = (v * groups + g) * MIX
                field[v, i, at : at + MIX, :] = value[start : start + MIX, t * LANES : (t + 1) * LANES] * units[v][0:1]

    def move(v, at):
        def above_flow(i, down):
            flows[v, i, pl.ds(at + 8, 8), :] = down
            return flows[v, i, pl.ds(at + 7, 8), :]

        pieces = [field[v, i, pl.ds(at, 8), :] for i in range(TILES)]
        below = [field[v, i, pl.ds(at + 1, 8), :] for i in range(TILES)]
        return advance(pieces, below, above_flow, GROUP)

    def empty(at):
        rows = [packed[at : at + 2 * MIX, g * WIDE : (g + 1) * WIDE] for g in range(groups)]
        value = jnp.dot(jnp.concatenate(rows, axis=0), gather[...], preferred_element_type=jnp.float32)
        value = value.astype(jnp.bfloat16)
        for g in range(groups):
            out_ref[at // 8 : (at + 2 * MIX) // 8, :, g * WIDE : (g + 1) * WIDE] = value[
                g * 2 * MIX : (g + 1) * 2 * MIX
            ].reshape(2 * MIX // 8, 8, WIDE)

    fill(0)
    for p in range(PASSES):
        for start in range(0, ROWS, MIX):
            if p == 0 and start + MIX < ROWS:
                fill(start + MIX)
            if p == PASSES - 1 and start:
                empty(2 * (start - MIX))
            for at in range(start, start + MIX, 8):
                new = [move(v, at) for v in range(2)]
                for i in range(TILES):
                    if p < PASSES - 1:
                        field[0, i, at : at + 8, :] = new[0][i]
                        field[1, i, at : at + 8, :] = new[1][i]
                    else:
                        a, b = new[0][i] * backs[0], new[1][i] * backs[1]
                        even = jnp.where(low, a, pltpu.roll(b, 4, 0))
                        odd = jnp.where(low, pltpu.roll(a, 4, 0), b)
                        both = jnp.concatenate([even, odd], axis=0).astype(jnp.bfloat16)
                        packed[2 * at : 2 * at + 16, i * LANES : (i + 1) * LANES] = both
    empty(2 * (ROWS - MIX))
    ends_ref[:, :16] = frames_ref[:, :16]
    ends_ref[:, 16:] = frames_ref[:, ROWS - 16 :]


def edge_kernel(kappa_ref, ends_ref, above_ref, under_ref, _, out_ref, sems, field, flows, blocks):
    strip = lax.axis_index("strip")
    inside = (
        jnp.where(strip == 0, 0.0, 1.0).astype(jnp.float32),
        jnp.where(strip == lax.axis_size("strip") - 1, 0.0, 1.0).astype(jnp.float32),
    )
    low = lax.broadcasted_iota(jnp.int32, (8, LANES), 0) < 4
    zero = jnp.zeros((8, LANES), jnp.float32)
    spots = [slice(i * LANES, (i + 1) * LANES) for i in range(TILES)]
    for n in range(4):
        for i in range(TILES):
            field[n, i, 16:24, :] = zero
            flows[n, i, 0:8, :] = zero
    done = []
    for v in range(2):
        unit = ROOT5 / jnp.full((1, LANES), kappa_ref[v], jnp.float32)
        sides = []
        for side in range(2):
            if side == 0:
                own = ends_ref[v, :16].astype(jnp.float32)[0:8]
                far = above_ref[v].astype(jnp.float32)
                window = [jnp.concatenate([far, far], axis=0), own]
            else:
                own = ends_ref[v, 16:].astype(jnp.float32)[8:16]
                far = under_ref[v].astype(jnp.float32)
                window = [own, jnp.concatenate([far, far], axis=0)]
            mid = [[w[:, s] * unit for s in spots] for w in window]
            for p in range(PASSES):
                for k in range(2):
                    for i in range(TILES):
                        field[2 * v + side, i, 8 * k : 8 * k + 8, :] = mid[k][i]
                for k in range(2):
                    below = [field[2 * v + side, i, 8 * k + 1 : 8 * k + 9, :] for i in range(TILES)]

                    def above_flow(i, down, at=8 * k, n=2 * v + side):
                        flows[n, i, at + 8 : at + 16, :] = down
                        return flows[n, i, at + 7 : at + 15, :]

                    mid[k] = advance(mid[k], below, above_flow, 1)
                mid[side] = [value * inside[side] for value in mid[side]]
            sides.append([value * (kappa_ref[v] * (1.0 / ROOT5)) for value in mid[1 - side]])
        done.append(sides)
    for i in range(TILES):
        top = jnp.where(low, done[0][0][i], pltpu.roll(done[1][0][i], 4, 0))
        end = jnp.where(low, pltpu.roll(done[0][1][i], 4, 0), done[1][1][i])
        blocks[0, :, spots[i]] = top.astype(jnp.bfloat16)
        blocks[1, :, spots[i]] = end.astype(jnp.bfloat16)
    copies = [
        pltpu.make_async_copy(blocks.at[0], out_ref.at[0], sems.at[0]),
        pltpu.make_async_copy(blocks.at[1], out_ref.at[63], sems.at[1]),
    ]
    for copy in copies:
        copy.start()
    for copy in copies:
        copy.wait()


def detrend_kernel(weights_ref, stored_ref, dff_ref, slope_ref, ratio):
    stored = stored_ref[...].reshape(4 * TIMES, CHUNK)
    for b, k in enumerate(STARTS):
        baseline = jnp.dot(
            weights_ref[128 * b : 128 * b + 128, :], stored[k : k + 256], preferred_element_type=jnp.float32
        )
        value = stored[128 * b : 128 * b + 128].astype(jnp.float32)
        ratio[16 * b : 16 * b + 16] = ((value - baseline) / (baseline + 0.1)).reshape(16, 8, CHUNK)

    low = lax.broadcasted_iota(jnp.int32, (8, LANES), 0) < 4
    for i in range(CHUNK // LANES):
        spot = slice(i * LANES, (i + 1) * LANES)
        own = ratio[0, :, spot]
        turned = pltpu.roll(own, 4, 0)
        previous = None
        for j in range(TIMES // 2):
            if j + 1 < TIMES // 2:
                other = ratio[j + 1, :, spot]
                other_turned = pltpu.roll(other, 4, 0)
                between = jnp.where(low, turned, other_turned)
            else:
                other = other_turned = None
                between = turned
            if previous is None:
                slope = jnp.where(low, between - own, 0.5 * (between - turned))
            elif other is None:
                slope = jnp.where(low, 0.5 * (between - previous), own - previous)
            else:
                slope = 0.5 * (between - previous)
            dff_ref[j, 0, :, spot] = own[0:4].astype(jnp.bfloat16)
            dff_ref[j, 1, :, spot] = turned[0:4].astype(jnp.bfloat16)
            slope_ref[j, 0, :, spot] = slope[0:4].astype(jnp.bfloat16)
            slope_ref[j, 1, :, spot] = pltpu.roll(slope, 4, 0)[0:4].astype(jnp.bfloat16)
            own, turned, previous = other, other_turned, between


VMEM = pl.BlockSpec(memory_space=pltpu.VMEM)
SMEM = pl.BlockSpec(memory_space=pltpu.SMEM)
ANY = pl.BlockSpec(memory_space=pl.ANY)


def diffuse(frames, kappa):
    devices = lax.axis_size("strip")
    up = [(i, i + 1) for i in range(devices - 1)]
    down = [(i + 1, i) for i in range(devices - 1)]
    above = lax.ppermute(frames[:, ROWS - HALO :], "strip", up)
    under = lax.ppermute(frames[:, :HALO], "strip", down)
    params = pltpu.CompilerParams(vmem_limit_bytes=24 * 1024 * 1024)
    inner, ends = pl.pallas_call(
        inner_kernel,
        out_shape=[
            jax.ShapeDtypeStruct((64, 8, 1024), jnp.bfloat16),
            jax.ShapeDtypeStruct((2, 32, 1024), jnp.bfloat16),
        ],
        in_specs=[SMEM, VMEM],
        out_specs=[VMEM, VMEM],
        scratch_shapes=[
            pltpu.VMEM((2, TILES, ROWS + 8, LANES), jnp.float32),
            pltpu.VMEM((2, TILES, ROWS + 8, LANES), jnp.float32),
            pltpu.VMEM((WIDE, WIDE), jnp.bfloat16),
            pltpu.VMEM((WIDE, WIDE), jnp.bfloat16),
            pltpu.VMEM((2 * ROWS, 1024), jnp.bfloat16),
        ],
        compiler_params=params,
        cost_estimate=pl.CostEstimate(flops=60_000_000, bytes_accessed=2 << 20, transcendentals=3 << 20),
        name="inner",
    )(kappa, frames)
    whole = pl.pallas_call(
        edge_kernel,
        out_shape=jax.ShapeDtypeStruct((64, 8, 1024), jnp.bfloat16),
        in_specs=[SMEM, VMEM, VMEM, VMEM, ANY],
        out_specs=ANY,
        scratch_shapes=[
            pltpu.SemaphoreType.DMA((2,)),
            pltpu.VMEM((4, TILES, 24, LANES), jnp.float32),
            pltpu.VMEM((4, TILES, 24, LANES), jnp.float32),
            pltpu.VMEM((2, 8, 1024), jnp.bfloat16),
        ],
        input_output_aliases={4: 0},
        compiler_params=params,
        name="edges",
    )(kappa, ends, above, under, inner)
    return whole


def detrend(stored):
    block = pl.BlockSpec((64, 2, 4, CHUNK), lambda i: (0, 0, 0, i))
    shape = jax.ShapeDtypeStruct((64, 2, 4, 1024), jnp.bfloat16)
    return pl.pallas_call(
        detrend_kernel,
        grid=(1024 // CHUNK,),
        out_shape=[shape, shape],
        in_specs=[pl.BlockSpec((512, 256), lambda i: (0, 0)), pl.BlockSpec((64, 8, CHUNK), lambda i: (0, 0, i))],
        out_specs=[block, block],
        scratch_shapes=[pltpu.VMEM((64, 8, CHUNK), jnp.float32)],
        compiler_params=pltpu.CompilerParams(vmem_limit_bytes=24 * 1024 * 1024),
        name="detrend",
    )(band_weights(), stored)


def local(frames, kappa):
    blocks = diffuse(frames.reshape(2, ROWS, 1024), kappa)
    stored = lax.all_to_all(blocks, "vol", split_axis=0, concat_axis=0, tiled=True)
    dff, slope = detrend(stored)
    return dff.reshape(128, 1, 4, 1, 1024), slope.reshape(128, 1, 4, 1, 1024)


def solution(mesh):
    out = P(None, None, "vol", "strip", None)
    return jax.shard_map(
        local,
        mesh=mesh,
        in_specs=(P("vol", None, "strip", None), P("vol")),
        out_specs=(out, out),
        check_vma=False,
    )
```

time: 71.7 us -> 67.2 us (0.937)
  Pallas kernels: 14.3 us -> 9.83 us
    pallas_call x2, Pallas kernels: 11.4 us -> 7.42 us  [the longest x1 6.09 us: diffuse(): pl.pallas_call(inner_kernel, out_shape=[jax.ShapeDtypeStruct((64, 8, 1024...]
  transfers between devices with their start and end apart: 2 -> 2, of which waited for: 0 -> 0; matrix products, arithmetic and copies ran while one was open for 0% -> 0% of each run, Pallas kernels for 14% -> 9%
where the time goes in v2:
time: 67.2 us; the launch traced here: 66.9 us
  blocking collectives  41.9 us (62%)
  starting transfers between devices  12.5 us (19%)
  Pallas kernels  9.83 us (15%)
  local copies, waits for them, and re-layouts  2.03 us (3%)
  between operations  0.71 us (1%)
    all_to_all x1, blocking collectives, local(): lax.all_to_all(blocks, 'vol', split_axis=0, concat_axis=0, tiled=True)  41.9 us
    ppermute x1, starting transfers between devices, diffuse(): above = lax.ppermute(frames[:, ROWS - HALO:], 'strip', up)  10 us
    pallas_call x1, Pallas kernels, diffuse(): pl.pallas_call(inner_kernel, out_shape=[jax.ShapeDtypeStruct((64, 8, 1024...  6.09 us
    ppermute x1, starting transfers between devices, diffuse(): under = lax.ppermute(frames[:, :HALO], 'strip', down)  2.46 us
    pallas_call x1, Pallas kernels, detrend(): pl.pallas_call(detrend_kernel, grid=(1024 // CHUNK,), out_shape=[shape, s...  2.41 us
  transfers between devices with their start and end apart: 2, of which 0 were waited for; matrix products, arithmetic and copies ran while one was open for 0% of the time, Pallas kernels for 9%

profile of v2, /device:TPU:7, one launch (start us, length us, event | category | flops | bytes accessed | tf_op | source)
XLA Modules:
  0.0 66.9 jit_solution(4316330740502683291)
XLA Ops:
  0.6 0.8 %fusion = (bf16[2,4,1024]{2,1,0:T(4,128)(2,1)S(1)}, bf16[2,4,1024]{2,1,0:T(4,128)(2,1)S(1)}) fusion(bf16[2,256,1024]{2,1,0:T(8,128)(2,1)} %bitcast.7), kind=kLoop, calls=%fused_computation | loop fusion | bytes 65536 | tf_op jit(solution)/shard_map/slice | solution.py:234
  1.4 0.0 copy-start.2
  1.4 2.5 %collective-permute-start.1 = (bf16[2,4,1024]{2,1,0:T(4,128)(2,1)S(1)}, bf16[2,4,1024]{2,1,0:T(4,128)(2,1)S(1)}, u32[]{:S(2)}, u32[]{:S(2)}) collective-permute-start(bf16[2,4,1024]{2,1,0:T(4,128)(2,1)S(1)} %get-tuple-element.12), channel_id=1, source_target_pairs={{1,0},{2,1},{3,2},{4,3},{5,4},{6,5},{7,6},{9,8},{10,9},{11,10},{12... | collective-permute-start | bytes 49160 | tf_op jit(solution)/shard_map/ppermute | solution.py:234
  3.9 10.0 %collective-permute-start = (bf16[2,4,1024]{2,1,0:T(4,128)(2,1)S(1)}, bf16[2,4,1024]{2,1,0:T(4,128)(2,1)S(1)}, u32[]{:S(2)}, u32[]{:S(2)}) collective-permute-start(bf16[2,4,1024]{2,1,0:T(4,128)(2,1)S(1)} %get-tuple-element.13), channel_id=1, source_target_pairs={{0,1},{1,2},{2,3},{3,4},{4,5},{5,6},{6,7},{8,9},{9,10},{10,11},{11... | collective-permute-start | bytes 49160 | tf_op jit(solution)/shard_map/ppermute | solution.py:233
  13.9 0.0 copy-done.2
  13.9 0.0 copy-start.1
  13.9 1.2 %copy-done.1 = bf16[2,1,256,1024]{3,2,1,0:T(8,128)(2,1)S(1)} copy-done((bf16[2,1,256,1024]{3,2,1,0:T(8,128)(2,1)S(1)}, bf16[2,1,256,1024]{3,2,1,0:T(8,128)(2,1)}, u32[]{:S(2)}) %copy-start.1) | copy-done | bytes 1048600
  15.2 6.1 %inner.1 = (bf16[64,8,1024]{2,1,0:T(8,128)(2,1)S(1)}, bf16[2,32,1024]{2,1,0:T(8,128)(2,1)S(1)}) custom-call(f32[2]{0:T(128)S(1)} %copy-done.2, bf16[2,256,1024]{2,1,0:T(8,128)(2,1)S(1)} %bitcast.8), custom_call_target="tpu_custom_call" | custom-call | flops 60000000 | bytes 2097152 | tf_op jit(solution)/shard_map/inner/pallas_call | solution.py:236
  21.3 0.0 collective-permute-done.1.under_ref
  21.3 0.0 collective-permute-done.above_ref
  21.3 1.3 %edges.1 = bf16[64,8,1024]{2,1,0:T(8,128)(2,1)S(1)} custom-call(f32[2]{0:T(128)S(1)} %copy-done.2, bf16[2,32,1024]{2,1,0:T(8,128)(2,1)S(1)} %get-tuple-element.6.ends_ref, bf16[2,4,1024]{2,1,0:T(4,128)(2,1)S(1)} %collective-permute-done.above_ref, bf16[2,4,1024]{2,1,0:T(4,128)(2,1)S(1)} %collective-permute-done.1.under_ref, ...), custom_call_target="tpu_custom_call", output_to_operand_aliasing={{}: (4, {})} | custom-call | tf_op jit(solution)/shard_map/edges/pallas_call | solution.py:255
  22.6 0.0 copy-start
  22.6 41.9 %all_to_all.5.stored_ref = bf16[64,8,1024]{2,1,0:T(8,128)(2,1)S(1)} all-to-all(bf16[64,8,1024]{2,1,0:T(8,128)(2,1)S(1)} %edges.1), channel_id=1, replica_groups=mesh['vol'=64,'strip'=8] {'vol'}, dimensions={0} | all-to-all | bytes 2097152 | tf_op jit(solution)/shard_map/all_to_all | solution.py:290
  64.5 0.0 copy-done
  64.5 2.4 %detrend.1 = (bf16[64,2,4,1024]{3,2,1,0:T(4,128)(2,1)}, bf16[64,2,4,1024]{3,2,1,0:T(4,128)(2,1)}) custom-call(bf16[512,256]{1,0:T(8,128)(2,1)S(1)} %copy-done, bf16[64,8,1024]{2,1,0:T(8,128)(2,1)S(1)} %all_to_all.5.stored_ref), custom_call_target="tpu_custom_call" | custom-call | tf_op jit(solution)/shard_map/detrend/pallas_call | solution.py:276
Async XLA Ops:
  1.4 12.5 %copy-start.2 = (f32[2]{0:T(128)S(1)}, f32[2]{0:T(128)}, u32[]{:S(2)}) copy-start(f32[2]{0:T(128)} %kappa_ref.3) | copy-start | bytes 28
  1.4 19.8 %collective-permute-start.1 = (bf16[2,4,1024]{2,1,0:T(4,128)(2,1)S(1)}, bf16[2,4,1024]{2,1,0:T(4,128)(2,1)S(1)}, u32[]{:S(2)}, u32[]{:S(2)}) collective-permute-start(bf16[2,4,1024]{2,1,0:T(4,128)(2,1)S(1)} %get-tuple-element.12), channel_id=1, source_target_pairs={{1,0},{2,1},{3,2},{4,3},{5,4},{6,5},{7,6},{9,8},{10,9},{11,10},{12... | collective-permute-start | bytes 49160 | tf_op jit(solution)/shard_map/ppermute | solution.py:234
  3.9 17.4 %collective-permute-start = (bf16[2,4,1024]{2,1,0:T(4,128)(2,1)S(1)}, bf16[2,4,1024]{2,1,0:T(4,128)(2,1)S(1)}, u32[]{:S(2)}, u32[]{:S(2)}) collective-permute-start(bf16[2,4,1024]{2,1,0:T(4,128)(2,1)S(1)} %get-tuple-element.13), channel_id=1, source_target_pairs={{0,1},{1,2},{2,3},{3,4},{4,5},{5,6},{6,7},{8,9},{9,10},{10,11},{11... | collective-permute-start | bytes 49160 | tf_op jit(solution)/shard_map/ppermute | solution.py:233
  13.9 1.2 %copy-start.1 = (bf16[2,1,256,1024]{3,2,1,0:T(8,128)(2,1)S(1)}, bf16[2,1,256,1024]{3,2,1,0:T(8,128)(2,1)}, u32[]{:S(2)}) copy-start(bf16[2,1,256,1024]{3,2,1,0:T(8,128)(2,1)} %param.3) | copy-start | bytes 3145732
  22.6 41.9 %copy-start = (bf16[512,256]{1,0:T(8,128)(2,1)S(1)}, bf16[512,256]{1,0:T(8,128)(2,1)}, u32[]{:S(2)}) copy-start(bf16[512,256]{1,0:T(8,128)(2,1)} %constant.2.clone.weights_ref) | copy-start | bytes 786436

commit v3 on v2

--- a/solution.py
+++ b/solution.py
@@ -128,8 +128,9 @@
     ends_ref[:, 16:] = frames_ref[:, ROWS - 16 :]
 
 
-def edge_kernel(kappa_ref, ends_ref, above_ref, under_ref, _, out_ref, sems, field, flows, blocks):
+def edge_kernel(kappa_ref, ends_ref, one_ref, two_ref, _, out_ref, sems, field, flows, blocks):
     strip = lax.axis_index("strip")
+    even = lax.rem(strip, 2) == 0
     inside = (
         jnp.where(strip == 0, 0.0, 1.0).astype(jnp.float32),
         jnp.where(strip == lax.axis_size("strip") - 1, 0.0, 1.0).astype(jnp.float32),
@@ -148,11 +149,11 @@
         for side in range(2):
             if side == 0:
                 own = ends_ref[v, :16].astype(jnp.float32)[0:8]
-                far = above_ref[v].astype(jnp.float32)
+                far = jnp.where(even, two_ref[v].astype(jnp.float32), one_ref[v].astype(jnp.float32))
                 window = [jnp.concatenate([far, far], axis=0), own]
             else:
                 own = ends_ref[v, 16:].astype(jnp.float32)[8:16]
-                far = under_ref[v].astype(jnp.float32)
+                far = jnp.where(even, one_ref[v].astype(jnp.float32), two_ref[v].astype(jnp.float32))
                 window = [own, jnp.concatenate([far, far], axis=0)]
             mid = [[w[:, s] * unit for s in spots] for w in window]
             for p in range(PASSES):
@@ -228,10 +229,13 @@
 
 def diffuse(frames, kappa):
     devices = lax.axis_size("strip")
-    up = [(i, i + 1) for i in range(devices - 1)]
-    down = [(i + 1, i) for i in range(devices - 1)]
-    above = lax.ppermute(frames[:, ROWS - HALO :], "strip", up)
-    under = lax.ppermute(frames[:, :HALO], "strip", down)
+    even = lax.rem(lax.axis_index("strip"), 2) == 0
+    top, bottom = frames[:, :HALO], frames[:, ROWS - HALO :]
+    first = [pair for i in range(0, devices - 1, 2) for pair in ((i, i + 1), (i + 1, i))]
+    second = [pair for i in range(1, devices - 1, 2) for pair in ((i, i + 1), (i + 1, i))]
+    one, two = lax.optimization_barrier((jnp.where(even, bottom, top), jnp.where(even, top, bottom)))
+    one = lax.ppermute(one, "strip", first)
+    two = lax.ppermute(two, "strip", second)
     params = pltpu.CompilerParams(vmem_limit_bytes=24 * 1024 * 1024)
     inner, ends = pl.pallas_call(
         inner_kernel,
@@ -266,7 +270,7 @@
         input_output_aliases={4: 0},
         compiler_params=params,
         name="edges",
-    )(kappa, ends, above, under, inner)
+    )(kappa, ends, one, two, inner)
     return whole
 
 

time: 67.2 us -> 66.9 us (level)
  blocking collectives: 41.9 us -> 40.4 us
  starting transfers between devices: 12.5 us -> 13.7 us
  other arithmetic: 0 us -> 0.8 us
  local copies, waits for them, and re-layouts: 2.03 us -> 1.23 us
    all_to_all x1, blocking collectives: 41.9 us -> 40.4 us  [local(): lax.all_to_all(blocks, 'vol', split_axis=0, concat_axis=0, tiled=True)]
    ppermute x2, starting transfers between devices: 12.5 us -> 13.7 us  [the longest x1 11.2 us: diffuse(): two = lax.ppermute(two, 'strip', second)]
    select_n x0 -> x1, other arithmetic: none -> 0.8 us  [diffuse(): jnp.where(even, top, bottom)]
    slice x1 -> x0, local copies, waits for them, and re-layouts: 0.79 us -> none  [diffuse(): under = lax.ppermute(frames[:, :HALO], 'strip', down)]
where the time goes in v3:
time: 66.9 us; the launch traced here: 66.6 us
  blocking collectives  40.4 us (60%)
  starting transfers between devices  13.7 us (20%)
  Pallas kernels  9.82 us (15%)
  local copies, waits for them, and re-layouts  1.23 us (2%)
  other arithmetic  0.8 us (1%)
  between operations  0.72 us (1%)
    all_to_all x1, blocking collectives, local(): lax.all_to_all(blocks, 'vol', split_axis=0, concat_axis=0, tiled=True)  40.4 us
    ppermute x1, starting transfers between devices, diffuse(): two = lax.ppermute(two, 'strip', second)  11.2 us
    pallas_call x1, Pallas kernels, diffuse(): pl.pallas_call(inner_kernel, out_shape=[jax.ShapeDtypeStruct((64, 8, 1024...  6.08 us
    ppermute x1, starting transfers between devices, diffuse(): one = lax.ppermute(one, 'strip', first)  2.46 us
    pallas_call x1, Pallas kernels, detrend(): pl.pallas_call(detrend_kernel, grid=(1024 // CHUNK,), out_shape=[shape, s...  2.41 us
  transfers between devices with their start and end apart: 2, of which 0 were waited for; matrix products, arithmetic and copies ran while one was open for 0% of the time, Pallas kernels for 9%

profile of v3, /device:TPU:7, one launch (start us, length us, event | category | flops | bytes accessed | tf_op | source)
XLA Modules:
  0.0 66.6 jit_solution(9635452631309608929)
XLA Ops:
  0.6 0.8 %broadcast_select_fusion = (bf16[2,4,1024]{2,1,0:T(4,128)(2,1)S(1)}, bf16[2,4,1024]{2,1,0:T(4,128)(2,1)S(1)}) fusion(pred[]{:T(512)S(6)} %eq.3, bf16[2,256,1024]{2,1,0:T(8,128)(2,1)} %bitcast.7), kind=kLoop, calls=%fused_computation | loop fusion | flops 16384 | bytes 65537 | tf_op jit(solution)/shard_map/jit(_where)/select_n | solution.py:236
  1.4 0.0 copy-start.2
  1.4 2.5 %collective-permute-start = (bf16[2,4,1024]{2,1,0:T(4,128)(2,1)S(1)}, bf16[2,4,1024]{2,1,0:T(4,128)(2,1)S(1)}, u32[]{:S(2)}, u32[]{:S(2)}) collective-permute-start(bf16[2,4,1024]{2,1,0:T(4,128)(2,1)S(1)} %get-tuple-element.9), channel_id=1, source_target_pairs={{0,1},{1,0},{2,3},{3,2},{4,5},{5,4},{6,7},{7,6},{8,9},{9,8},{10,11... | collective-permute-start | bytes 49160 | tf_op jit(solution)/shard_map/ppermute | solution.py:237
  3.9 11.2 %collective-permute-start.1 = (bf16[2,4,1024]{2,1,0:T(4,128)(2,1)S(1)}, bf16[2,4,1024]{2,1,0:T(4,128)(2,1)S(1)}, u32[]{:S(2)}, u32[]{:S(2)}) collective-permute-start(bf16[2,4,1024]{2,1,0:T(4,128)(2,1)S(1)} %get-tuple-element.10), channel_id=1, source_target_pairs={{1,2},{2,1},{3,4},{4,3},{5,6},{6,5},{9,10},{10,9},{11,12},{12,11},... | collective-permute-start | bytes 49160 | tf_op jit(solution)/shard_map/ppermute | solution.py:238
  15.1 0.0 copy-done.2
  15.1 0.0 copy-start.1
  15.2 1.2 %copy-done.1 = bf16[2,1,256,1024]{3,2,1,0:T(8,128)(2,1)S(1)} copy-done((bf16[2,1,256,1024]{3,2,1,0:T(8,128)(2,1)S(1)}, bf16[2,1,256,1024]{3,2,1,0:T(8,128)(2,1)}, u32[]{:S(2)}) %copy-start.1) | copy-done | bytes 1048600
  16.4 6.1 %inner.1 = (bf16[64,8,1024]{2,1,0:T(8,128)(2,1)S(1)}, bf16[2,32,1024]{2,1,0:T(8,128)(2,1)S(1)}) custom-call(f32[2]{0:T(128)S(1)} %copy-done.2, bf16[2,256,1024]{2,1,0:T(8,128)(2,1)S(1)} %bitcast.8), custom_call_target="tpu_custom_call" | custom-call | flops 60000000 | bytes 2097152 | tf_op jit(solution)/shard_map/inner/pallas_call | solution.py:240
  22.5 0.0 collective-permute-done.one_ref
  22.5 0.0 collective-permute-done.1.two_ref
  22.5 1.3 %edges.1 = bf16[64,8,1024]{2,1,0:T(8,128)(2,1)S(1)} custom-call(f32[2]{0:T(128)S(1)} %copy-done.2, bf16[2,32,1024]{2,1,0:T(8,128)(2,1)S(1)} %get-tuple-element.8.ends_ref, bf16[2,4,1024]{2,1,0:T(4,128)(2,1)S(1)} %collective-permute-done.one_ref, bf16[2,4,1024]{2,1,0:T(4,128)(2,1)S(1)} %collective-permute-done.1.two_ref, ...), custom_call_target="tpu_custom_call", output_to_operand_aliasing={{}: (4, {})} | custom-call | tf_op jit(solution)/shard_map/edges/pallas_call | solution.py:259
  23.8 0.0 copy-start
  23.8 40.4 %all_to_all.5.stored_ref = bf16[64,8,1024]{2,1,0:T(8,128)(2,1)S(1)} all-to-all(bf16[64,8,1024]{2,1,0:T(8,128)(2,1)S(1)} %edges.1), channel_id=1, replica_groups=mesh['vol'=64,'strip'=8] {'vol'}, dimensions={0} | all-to-all | bytes 2097152 | tf_op jit(solution)/shard_map/all_to_all | solution.py:294
  64.2 0.0 copy-done
  64.2 2.4 %detrend.1 = (bf16[64,2,4,1024]{3,2,1,0:T(4,128)(2,1)}, bf16[64,2,4,1024]{3,2,1,0:T(4,128)(2,1)}) custom-call(bf16[512,256]{1,0:T(8,128)(2,1)S(1)} %copy-done, bf16[64,8,1024]{2,1,0:T(8,128)(2,1)S(1)} %all_to_all.5.stored_ref), custom_call_target="tpu_custom_call" | custom-call | tf_op jit(solution)/shard_map/detrend/pallas_call | solution.py:280
Async XLA Ops:
  1.4 13.7 %copy-start.2 = (f32[2]{0:T(128)S(1)}, f32[2]{0:T(128)}, u32[]{:S(2)}) copy-start(f32[2]{0:T(128)} %kappa_ref.3) | copy-start | bytes 28
  1.4 21.0 %collective-permute-start = (bf16[2,4,1024]{2,1,0:T(4,128)(2,1)S(1)}, bf16[2,4,1024]{2,1,0:T(4,128)(2,1)S(1)}, u32[]{:S(2)}, u32[]{:S(2)}) collective-permute-start(bf16[2,4,1024]{2,1,0:T(4,128)(2,1)S(1)} %get-tuple-element.9), channel_id=1, source_target_pairs={{0,1},{1,0},{2,3},{3,2},{4,5},{5,4},{6,7},{7,6},{8,9},{9,8},{10,11... | collective-permute-start | bytes 49160 | tf_op jit(solution)/shard_map/ppermute | solution.py:237
  3.9 18.6 %collective-permute-start.1 = (bf16[2,4,1024]{2,1,0:T(4,128)(2,1)S(1)}, bf16[2,4,1024]{2,1,0:T(4,128)(2,1)S(1)}, u32[]{:S(2)}, u32[]{:S(2)}) collective-permute-start(bf16[2,4,1024]{2,1,0:T(4,128)(2,1)S(1)} %get-tuple-element.10), channel_id=1, source_target_pairs={{1,2},{2,1},{3,4},{4,3},{5,6},{6,5},{9,10},{10,9},{11,12},{12,11},... | collective-permute-start | bytes 49160 | tf_op jit(solution)/shard_map/ppermute | solution.py:238
  15.1 1.2 %copy-start.1 = (bf16[2,1,256,1024]{3,2,1,0:T(8,128)(2,1)S(1)}, bf16[2,1,256,1024]{3,2,1,0:T(8,128)(2,1)}, u32[]{:S(2)}) copy-start(bf16[2,1,256,1024]{3,2,1,0:T(8,128)(2,1)} %param.3) | copy-start | bytes 3145732
  23.8 40.4 %copy-start = (bf16[512,256]{1,0:T(8,128)(2,1)S(1)}, bf16[512,256]{1,0:T(8,128)(2,1)}, u32[]{:S(2)}) copy-start(bf16[512,256]{1,0:T(8,128)(2,1)} %constant.12.clone.weights_ref) | copy-start | bytes 786436

commit v4 on v3

--- a/solution.py
+++ b/solution.py
@@ -128,7 +128,7 @@
     ends_ref[:, 16:] = frames_ref[:, ROWS - 16 :]
 
 
-def edge_kernel(kappa_ref, ends_ref, one_ref, two_ref, _, out_ref, sems, field, flows, blocks):
+def edge_kernel(kappa_ref, ends_ref, two_ref, one_ref, _, out_ref, sems, field, flows, blocks):
     strip = lax.axis_index("strip")
     even = lax.rem(strip, 2) == 0
     inside = (
@@ -233,9 +233,9 @@
     top, bottom = frames[:, :HALO], frames[:, ROWS - HALO :]
     first = [pair for i in range(0, devices - 1, 2) for pair in ((i, i + 1), (i + 1, i))]
     second = [pair for i in range(1, devices - 1, 2) for pair in ((i, i + 1), (i + 1, i))]
-    one, two = lax.optimization_barrier((jnp.where(even, bottom, top), jnp.where(even, top, bottom)))
+    two, one = lax.optimization_barrier((jnp.where(even, top, bottom), jnp.where(even, bottom, top)))
+    two = lax.ppermute(two, "strip", second)
     one = lax.ppermute(one, "strip", first)
-    two = lax.ppermute(two, "strip", second)
     params = pltpu.CompilerParams(vmem_limit_bytes=24 * 1024 * 1024)
     inner, ends = pl.pallas_call(
         inner_kernel,
@@ -270,7 +270,7 @@
         input_output_aliases={4: 0},
         compiler_params=params,
         name="edges",
-    )(kappa, ends, one, two, inner)
+    )(kappa, ends, two, one, inner)
     return whole
 
 

time: 66.9 us -> 66.6 us (level)
  the two profiles are of different devices: /device:TPU:7 before, /device:TPU:5 now
where the time goes in v4:
time: 66.6 us; the launch traced here: 66.3 us
  blocking collectives  40.4 us (61%)
  starting transfers between devices  13.4 us (20%)
  Pallas kernels  9.82 us (15%)
  local copies, waits for them, and re-layouts  1.23 us (2%)
  other arithmetic  0.8 us (1%)
  between operations  0.72 us (1%)
    all_to_all x1, blocking collectives, local(): lax.all_to_all(blocks, 'vol', split_axis=0, concat_axis=0, tiled=True)  40.4 us
    ppermute x1, starting transfers between devices, diffuse(): one = lax.ppermute(one, 'strip', first)  11.2 us
    pallas_call x1, Pallas kernels, diffuse(): pl.pallas_call(inner_kernel, out_shape=[jax.ShapeDtypeStruct((64, 8, 1024...  6.08 us
    pallas_call x1, Pallas kernels, detrend(): pl.pallas_call(detrend_kernel, grid=(1024 // CHUNK,), out_shape=[shape, s...  2.41 us
    ppermute x1, starting transfers between devices, diffuse(): two = lax.ppermute(two, 'strip', second)  2.16 us
  transfers between devices with their start and end apart: 2, of which 0 were waited for; matrix products, arithmetic and copies ran while one was open for 0% of the time, Pallas kernels for 9%

profile of v4, /device:TPU:5, one launch (start us, length us, event | category | flops | bytes accessed | tf_op | source)
XLA Modules:
  0.0 66.3 jit_solution(8970189406831123579)
XLA Ops:
  0.6 0.8 %broadcast_select_fusion = (bf16[2,4,1024]{2,1,0:T(4,128)(2,1)S(1)}, bf16[2,4,1024]{2,1,0:T(4,128)(2,1)S(1)}) fusion(pred[]{:T(512)S(6)} %eq.3, bf16[2,256,1024]{2,1,0:T(8,128)(2,1)} %bitcast.7), kind=kLoop, calls=%fused_computation | loop fusion | flops 16384 | bytes 65537 | tf_op jit(solution)/shard_map/jit(_where)/select_n | solution.py:236
  1.4 0.0 copy-start.2
  1.5 2.2 %collective-permute-start = (bf16[2,4,1024]{2,1,0:T(4,128)(2,1)S(1)}, bf16[2,4,1024]{2,1,0:T(4,128)(2,1)S(1)}, u32[]{:S(2)}, u32[]{:S(2)}) collective-permute-start(bf16[2,4,1024]{2,1,0:T(4,128)(2,1)S(1)} %get-tuple-element.9), channel_id=1, source_target_pairs={{1,2},{2,1},{3,4},{4,3},{5,6},{6,5},{9,10},{10,9},{11,12},{12,11},... | collective-permute-start | bytes 49160 | tf_op jit(solution)/shard_map/ppermute | solution.py:237
  3.6 11.2 %collective-permute-start.1 = (bf16[2,4,1024]{2,1,0:T(4,128)(2,1)S(1)}, bf16[2,4,1024]{2,1,0:T(4,128)(2,1)S(1)}, u32[]{:S(2)}, u32[]{:S(2)}) collective-permute-start(bf16[2,4,1024]{2,1,0:T(4,128)(2,1)S(1)} %get-tuple-element.10), channel_id=1, source_target_pairs={{0,1},{1,0},{2,3},{3,2},{4,5},{5,4},{6,7},{7,6},{8,9},{9,8},{10,11... | collective-permute-start | bytes 49160 | tf_op jit(solution)/shard_map/ppermute | solution.py:238
  14.8 0.0 copy-done.2
  14.9 0.0 copy-start.1
  14.9 1.2 %copy-done.1 = bf16[2,1,256,1024]{3,2,1,0:T(8,128)(2,1)S(1)} copy-done((bf16[2,1,256,1024]{3,2,1,0:T(8,128)(2,1)S(1)}, bf16[2,1,256,1024]{3,2,1,0:T(8,128)(2,1)}, u32[]{:S(2)}) %copy-start.1) | copy-done | bytes 1048600
  16.1 6.1 %inner.1 = (bf16[64,8,1024]{2,1,0:T(8,128)(2,1)S(1)}, bf16[2,32,1024]{2,1,0:T(8,128)(2,1)S(1)}) custom-call(f32[2]{0:T(128)S(1)} %copy-done.2, bf16[2,256,1024]{2,1,0:T(8,128)(2,1)S(1)} %bitcast.8), custom_call_target="tpu_custom_call" | custom-call | flops 60000000 | bytes 2097152 | tf_op jit(solution)/shard_map/inner/pallas_call | solution.py:240
  22.2 0.0 collective-permute-done.two_ref
  22.2 0.0 collective-permute-done.1.one_ref
  22.2 1.3 %edges.1 = bf16[64,8,1024]{2,1,0:T(8,128)(2,1)S(1)} custom-call(f32[2]{0:T(128)S(1)} %copy-done.2, bf16[2,32,1024]{2,1,0:T(8,128)(2,1)S(1)} %get-tuple-element.8.ends_ref, bf16[2,4,1024]{2,1,0:T(4,128)(2,1)S(1)} %collective-permute-done.two_ref, bf16[2,4,1024]{2,1,0:T(4,128)(2,1)S(1)} %collective-permute-done.1.one_ref, ...), custom_call_target="tpu_custom_call", output_to_operand_aliasing={{}: (4, {})} | custom-call | tf_op jit(solution)/shard_map/edges/pallas_call | solution.py:259
  23.5 0.0 copy-start
  23.5 40.4 %all_to_all.5.stored_ref = bf16[64,8,1024]{2,1,0:T(8,128)(2,1)S(1)} all-to-all(bf16[64,8,1024]{2,1,0:T(8,128)(2,1)S(1)} %edges.1), channel_id=1, replica_groups=mesh['vol'=64,'strip'=8] {'vol'}, dimensions={0} | all-to-all | bytes 2097152 | tf_op jit(solution)/shard_map/all_to_all | solution.py:294
  63.9 0.0 copy-done
  63.9 2.4 %detrend.1 = (bf16[64,2,4,1024]{3,2,1,0:T(4,128)(2,1)}, bf16[64,2,4,1024]{3,2,1,0:T(4,128)(2,1)}) custom-call(bf16[512,256]{1,0:T(8,128)(2,1)S(1)} %copy-done, bf16[64,8,1024]{2,1,0:T(8,128)(2,1)S(1)} %all_to_all.5.stored_ref), custom_call_target="tpu_custom_call" | custom-call | tf_op jit(solution)/shard_map/detrend/pallas_call | solution.py:280
Async XLA Ops:
  1.4 13.4 %copy-start.2 = (f32[2]{0:T(128)S(1)}, f32[2]{0:T(128)}, u32[]{:S(2)}) copy-start(f32[2]{0:T(128)} %kappa_ref.3) | copy-start | bytes 28
  1.5 20.7 %collective-permute-start = (bf16[2,4,1024]{2,1,0:T(4,128)(2,1)S(1)}, bf16[2,4,1024]{2,1,0:T(4,128)(2,1)S(1)}, u32[]{:S(2)}, u32[]{:S(2)}) collective-permute-start(bf16[2,4,1024]{2,1,0:T(4,128)(2,1)S(1)} %get-tuple-element.9), channel_id=1, source_target_pairs={{1,2},{2,1},{3,4},{4,3},{5,6},{6,5},{9,10},{10,9},{11,12},{12,11},... | collective-permute-start | bytes 49160 | tf_op jit(solution)/shard_map/ppermute | solution.py:237
  3.6 18.6 %collective-permute-start.1 = (bf16[2,4,1024]{2,1,0:T(4,128)(2,1)S(1)}, bf16[2,4,1024]{2,1,0:T(4,128)(2,1)S(1)}, u32[]{:S(2)}, u32[]{:S(2)}) collective-permute-start(bf16[2,4,1024]{2,1,0:T(4,128)(2,1)S(1)} %get-tuple-element.10), channel_id=1, source_target_pairs={{0,1},{1,0},{2,3},{3,2},{4,5},{5,4},{6,7},{7,6},{8,9},{9,8},{10,11... | collective-permute-start | bytes 49160 | tf_op jit(solution)/shard_map/ppermute | solution.py:238
  14.9 1.2 %copy-start.1 = (bf16[2,1,256,1024]{3,2,1,0:T(8,128)(2,1)S(1)}, bf16[2,1,256,1024]{3,2,1,0:T(8,128)(2,1)}, u32[]{:S(2)}) copy-start(bf16[2,1,256,1024]{3,2,1,0:T(8,128)(2,1)} %param.3) | copy-start | bytes 3145732
  23.5 40.4 %copy-start = (bf16[512,256]{1,0:T(8,128)(2,1)S(1)}, bf16[512,256]{1,0:T(8,128)(2,1)}, u32[]{:S(2)}) copy-start(bf16[512,256]{1,0:T(8,128)(2,1)} %constant.12.clone.weights_ref) | copy-start | bytes 786436

commit v5 on v2

--- a/solution.py
+++ b/solution.py
@@ -21,6 +21,16 @@
 STARTS = (0, 64, 192, 256)
 CHUNK = 512
 ROOT5 = math.sqrt(5.0)
+
+
+ROUNDS = ((0, 2, 5), (1, 3), (4, 6))
+
+
+def is_upper(strip, uppers):
+    found = strip == uppers[0]
+    for i in uppers[1:]:
+        found = found | (strip == i)
+    return found
 
 
 def band_weights():
@@ -128,8 +138,9 @@
     ends_ref[:, 16:] = frames_ref[:, ROWS - 16 :]
 
 
-def edge_kernel(kappa_ref, ends_ref, above_ref, under_ref, _, out_ref, sems, field, flows, blocks):
+def edge_kernel(kappa_ref, ends_ref, one_ref, two_ref, three_ref, _, out_ref, sems, field, flows, blocks):
     strip = lax.axis_index("strip")
+    got = [(is_upper(strip, r), ref) for r, ref in zip(ROUNDS, (one_ref, two_ref, three_ref))]
     inside = (
         jnp.where(strip == 0, 0.0, 1.0).astype(jnp.float32),
         jnp.where(strip == lax.axis_size("strip") - 1, 0.0, 1.0).astype(jnp.float32),
@@ -148,11 +159,11 @@
         for side in range(2):
             if side == 0:
                 own = ends_ref[v, :16].astype(jnp.float32)[0:8]
-                far = above_ref[v].astype(jnp.float32)
+                far = sum(jnp.where(upper, 0.0, ref[v].astype(jnp.float32)) for upper, ref in got)
                 window = [jnp.concatenate([far, far], axis=0), own]
             else:
                 own = ends_ref[v, 16:].astype(jnp.float32)[8:16]
-                far = under_ref[v].astype(jnp.float32)
+                far = sum(jnp.where(upper, ref[v].astype(jnp.float32), 0.0) for upper, ref in got)
                 window = [own, jnp.concatenate([far, far], axis=0)]
             mid = [[w[:, s] * unit for s in spots] for w in window]
             for p in range(PASSES):
@@ -227,11 +238,11 @@
 
 
 def diffuse(frames, kappa):
-    devices = lax.axis_size("strip")
-    up = [(i, i + 1) for i in range(devices - 1)]
-    down = [(i + 1, i) for i in range(devices - 1)]
-    above = lax.ppermute(frames[:, ROWS - HALO :], "strip", up)
-    under = lax.ppermute(frames[:, :HALO], "strip", down)
+    top, bottom = frames[:, :HALO], frames[:, ROWS - HALO :]
+    strip = lax.axis_index("strip")
+    sent = lax.optimization_barrier(tuple(jnp.where(is_upper(strip, r), bottom, top) for r in ROUNDS))
+    swaps = [[pair for i in r for pair in ((i, i + 1), (i + 1, i))] for r in ROUNDS]
+    got = [lax.ppermute(rows, "strip", swap) for rows, swap in zip(sent, swaps)]
     params = pltpu.CompilerParams(vmem_limit_bytes=24 * 1024 * 1024)
     inner, ends = pl.pallas_call(
         inner_kernel,
@@ -255,7 +266,7 @@
     whole = pl.pallas_call(
         edge_kernel,
         out_shape=jax.ShapeDtypeStruct((64, 8, 1024), jnp.bfloat16),
-        in_specs=[SMEM, VMEM, VMEM, VMEM, ANY],
+        in_specs=[SMEM, VMEM, VMEM, VMEM, VMEM, ANY],
         out_specs=ANY,
         scratch_shapes=[
             pltpu.SemaphoreType.DMA((2,)),
@@ -263,10 +274,10 @@
             pltpu.VMEM((4, TILES, 24, LANES), jnp.float32),
             pltpu.VMEM((2, 8, 1024), jnp.bfloat16),
         ],
-        input_output_aliases={4: 0},
+        input_output_aliases={5: 0},
         compiler_params=params,
         name="edges",
-    )(kappa, ends, above, under, inner)
+    )(kappa, ends, *got, inner)
     return whole
 
 

time: 67.2 us -> 64.9 us (0.966)
  blocking collectives: 41.9 us -> 40.1 us
  other arithmetic: 0 us -> 0.81 us
  local copies, waits for them, and re-layouts: 2.03 us -> 1.23 us
    all_to_all x1, blocking collectives: 41.9 us -> 40.1 us  [local(): lax.all_to_all(blocks, 'vol', split_axis=0, concat_axis=0, tiled=True)]
    select_n x0 -> x1, other arithmetic: none -> 0.81 us  [diffuse(): jnp.where(is_upper(strip, r), bottom, top)]
    slice x1 -> x0, local copies, waits for them, and re-layouts: 0.79 us -> none  [diffuse(): under = lax.ppermute(frames[:, :HALO], 'strip', down)]
    ppermute x2 -> x3, starting transfers between devices: 12.5 us -> 11.9 us  [diffuse(): got = [lax.ppermute(rows, 'strip', swap) for rows, swap in zip(sent, swaps)]]
  transfers between devices with their start and end apart: 2 -> 3, of which waited for: 0 -> 0; matrix products, arithmetic and copies ran while one was open for 0% -> 0% of each run, Pallas kernels for 9% -> 9%
where the time goes in v5:
time: 64.9 us; the launch traced here: 64.6 us
  blocking collectives  40.1 us (62%)
  starting transfers between devices  11.9 us (18%)
  Pallas kernels  9.83 us (15%)
  local copies, waits for them, and re-layouts  1.23 us (2%)
  other arithmetic  0.81 us (1%)
  between operations  0.75 us (1%)
    all_to_all x1, blocking collectives, local(): lax.all_to_all(blocks, 'vol', split_axis=0, concat_axis=0, tiled=True)  40.1 us
    ppermute x3, starting transfers between devices, diffuse(): got = [lax.ppermute(rows, 'strip', swap) for rows, swap in zip(sent, swaps)]  11.9 us
    pallas_call x1, Pallas kernels, diffuse(): pl.pallas_call(inner_kernel, out_shape=[jax.ShapeDtypeStruct((64, 8, 1024...  6.09 us
    pallas_call x1, Pallas kernels, detrend(): pl.pallas_call(detrend_kernel, grid=(1024 // CHUNK,), out_shape=[shape, s...  2.41 us
    pallas_call x1, Pallas kernels, diffuse(): pl.pallas_call(edge_kernel, out_shape=jax.ShapeDtypeStruct((64, 8, 1024),...  1.33 us
  transfers between devices with their start and end apart: 3, of which 0 were waited for; matrix products, arithmetic and copies ran while one was open for 0% of the time, Pallas kernels for 9%

profile of v5, /device:TPU:7, one launch (start us, length us, event | category | flops | bytes accessed | tf_op | source)
XLA Modules:
  0.0 64.6 jit_solution(6457451659863696176)
XLA Ops:
  0.7 0.8 %broadcast_select_fusion = (bf16[2,4,1024]{2,1,0:T(4,128)(2,1)S(1)}, bf16[2,4,1024]{2,1,0:T(4,128)(2,1)S(1)}, bf16[2,4,1024]{2,1,0:T(4,128)(2,1)S(1)}) fusion(pred[]{:T(512)S(6)} %or.15, bf16[2,256,1024]{2,1,0:T(8,128)(2,1)} %bitcast.7, pred[]{:T(512)S(6)} %or.13, pred[]{:T(512)S(6)} %or.14), kind=kLoop, calls=%fused_computation | loop fusion | flops 24576 | bytes 81923 | tf_op jit(solution)/shard_map/jit(_where)/select_n | solution.py:243
  1.5 0.0 copy-start.2
  1.5 2.5 %collective-permute-start = (bf16[2,4,1024]{2,1,0:T(4,128)(2,1)S(1)}, bf16[2,4,1024]{2,1,0:T(4,128)(2,1)S(1)}, u32[]{:S(2)}, u32[]{:S(2)}) collective-permute-start(bf16[2,4,1024]{2,1,0:T(4,128)(2,1)S(1)} %get-tuple-element.10), channel_id=1, source_target_pairs={{0,1},{1,0},{2,3},{3,2},{5,6},{6,5},{8,9},{9,8},{10,11},{11,10},{1... | collective-permute-start | bytes 49160 | tf_op jit(solution)/shard_map/ppermute | solution.py:245
  3.9 8.8 %collective-permute-start.1 = (bf16[2,4,1024]{2,1,0:T(4,128)(2,1)S(1)}, bf16[2,4,1024]{2,1,0:T(4,128)(2,1)S(1)}, u32[]{:S(2)}, u32[]{:S(2)}) collective-permute-start(bf16[2,4,1024]{2,1,0:T(4,128)(2,1)S(1)} %get-tuple-element.11), channel_id=1, source_target_pairs={{1,2},{2,1},{3,4},{4,3},{9,10},{10,9},{11,12},{12,11},{17,18},{18,... | collective-permute-start | bytes 49160 | tf_op jit(solution)/shard_map/ppermute | solution.py:245
  12.7 0.7 %collective-permute-start.2 = (bf16[2,4,1024]{2,1,0:T(4,128)(2,1)S(1)}, bf16[2,4,1024]{2,1,0:T(4,128)(2,1)S(1)}, u32[]{:S(2)}, u32[]{:S(2)}) collective-permute-start(bf16[2,4,1024]{2,1,0:T(4,128)(2,1)S(1)} %get-tuple-element.12), channel_id=1, source_target_pairs={{4,5},{5,4},{6,7},{7,6},{12,13},{13,12},{14,15},{15,14},{20,21},{2... | collective-permute-start | bytes 49160 | tf_op jit(solution)/shard_map/ppermute | solution.py:245
  13.4 0.0 copy-done.2
  13.4 0.0 copy-start.1
  13.4 1.2 %copy-done.1 = bf16[2,1,256,1024]{3,2,1,0:T(8,128)(2,1)S(1)} copy-done((bf16[2,1,256,1024]{3,2,1,0:T(8,128)(2,1)S(1)}, bf16[2,1,256,1024]{3,2,1,0:T(8,128)(2,1)}, u32[]{:S(2)}) %copy-start.1) | copy-done | bytes 1048600
  14.6 6.1 %inner.1 = (bf16[64,8,1024]{2,1,0:T(8,128)(2,1)S(1)}, bf16[2,32,1024]{2,1,0:T(8,128)(2,1)S(1)}) custom-call(f32[2]{0:T(128)S(1)} %copy-done.2, bf16[2,256,1024]{2,1,0:T(8,128)(2,1)S(1)} %bitcast.8), custom_call_target="tpu_custom_call" | custom-call | flops 60000000 | bytes 2097152 | tf_op jit(solution)/shard_map/inner/pallas_call | solution.py:247
  20.7 0.0 collective-permute-done.one_ref
  20.7 0.0 collective-permute-done.1.two_ref
  20.7 0.0 collective-permute-done.2.three_ref
  20.7 1.3 %edges.1 = bf16[64,8,1024]{2,1,0:T(8,128)(2,1)S(1)} custom-call(f32[2]{0:T(128)S(1)} %copy-done.2, bf16[2,32,1024]{2,1,0:T(8,128)(2,1)S(1)} %get-tuple-element.9.ends_ref, bf16[2,4,1024]{2,1,0:T(4,128)(2,1)S(1)} %collective-permute-done.one_ref, bf16[2,4,1024]{2,1,0:T(4,128)(2,1)S(1)} %collective-permute-done.1.two_ref, ...), custom_call_target="tpu_custom_call", output_to_operand_aliasing={{}: (5, {})} | custom-call | tf_op jit(solution)/shard_map/edges/pallas_call | solution.py:266
  22.1 0.0 copy-start
  22.1 40.1 %all_to_all.5.stored_ref = bf16[64,8,1024]{2,1,0:T(8,128)(2,1)S(1)} all-to-all(bf16[64,8,1024]{2,1,0:T(8,128)(2,1)S(1)} %edges.1), channel_id=1, replica_groups=mesh['vol'=64,'strip'=8] {'vol'}, dimensions={0} | all-to-all | bytes 2097152 | tf_op jit(solution)/shard_map/all_to_all | solution.py:301
  62.2 0.0 copy-done
  62.2 2.4 %detrend.1 = (bf16[64,2,4,1024]{3,2,1,0:T(4,128)(2,1)}, bf16[64,2,4,1024]{3,2,1,0:T(4,128)(2,1)}) custom-call(bf16[512,256]{1,0:T(8,128)(2,1)S(1)} %copy-done, bf16[64,8,1024]{2,1,0:T(8,128)(2,1)S(1)} %all_to_all.5.stored_ref), custom_call_target="tpu_custom_call" | custom-call | tf_op jit(solution)/shard_map/detrend/pallas_call | solution.py:287
Async XLA Ops:
  1.5 11.9 %copy-start.2 = (f32[2]{0:T(128)S(1)}, f32[2]{0:T(128)}, u32[]{:S(2)}) copy-start(f32[2]{0:T(128)} %kappa_ref.3) | copy-start | bytes 28
  1.5 19.2 %collective-permute-start = (bf16[2,4,1024]{2,1,0:T(4,128)(2,1)S(1)}, bf16[2,4,1024]{2,1,0:T(4,128)(2,1)S(1)}, u32[]{:S(2)}, u32[]{:S(2)}) collective-permute-start(bf16[2,4,1024]{2,1,0:T(4,128)(2,1)S(1)} %get-tuple-element.10), channel_id=1, source_target_pairs={{0,1},{1,0},{2,3},{3,2},{5,6},{6,5},{8,9},{9,8},{10,11},{11,10},{1... | collective-permute-start | bytes 49160 | tf_op jit(solution)/shard_map/ppermute | solution.py:245
  3.9 16.8 %collective-permute-start.1 = (bf16[2,4,1024]{2,1,0:T(4,128)(2,1)S(1)}, bf16[2,4,1024]{2,1,0:T(4,128)(2,1)S(1)}, u32[]{:S(2)}, u32[]{:S(2)}) collective-permute-start(bf16[2,4,1024]{2,1,0:T(4,128)(2,1)S(1)} %get-tuple-element.11), channel_id=1, source_target_pairs={{1,2},{2,1},{3,4},{4,3},{9,10},{10,9},{11,12},{12,11},{17,18},{18,... | collective-permute-start | bytes 49160 | tf_op jit(solution)/shard_map/ppermute | solution.py:245
  12.7 8.0 %collective-permute-start.2 = (bf16[2,4,1024]{2,1,0:T(4,128)(2,1)S(1)}, bf16[2,4,1024]{2,1,0:T(4,128)(2,1)S(1)}, u32[]{:S(2)}, u32[]{:S(2)}) collective-permute-start(bf16[2,4,1024]{2,1,0:T(4,128)(2,1)S(1)} %get-tuple-element.12), channel_id=1, source_target_pairs={{4,5},{5,4},{6,7},{7,6},{12,13},{13,12},{14,15},{15,14},{20,21},{2... | collective-permute-start | bytes 49160 | tf_op jit(solution)/shard_map/ppermute | solution.py:245
  13.4 1.2 %copy-start.1 = (bf16[2,1,256,1024]{3,2,1,0:T(8,128)(2,1)S(1)}, bf16[2,1,256,1024]{3,2,1,0:T(8,128)(2,1)}, u32[]{:S(2)}) copy-start(bf16[2,1,256,1024]{3,2,1,0:T(8,128)(2,1)} %param.3) | copy-start | bytes 3145732
  22.1 40.1 %copy-start = (bf16[512,256]{1,0:T(8,128)(2,1)S(1)}, bf16[512,256]{1,0:T(8,128)(2,1)}, u32[]{:S(2)}) copy-start(bf16[512,256]{1,0:T(8,128)(2,1)} %constant.20.clone.weights_ref) | copy-start | bytes 786436
